TPU v7x, 128 devices: a whole 4x4x4 slice. The times are simulated.
128 devices in a mesh: gx: 16 (over x, z), gy: 8 (over y, core).
Axes of the slice: x: 4, y: 4, z: 4, core: 2. Of those that a mesh axis runs over, the one named last changes fastest.
Arguments:
- density: float32 [16, 8, 8, 64, 1024], P('gx', 'gy'), may hold values from -0.07 to 1.15
- moves: int32 [16, 8, 8], P('gx', 'gy'), may hold values from 0 to 1023, as said below
- cols: int32 [16, 8, 8, 16], P('gx', 'gy'), may hold values from 0 to 39, as said below
- halo_rows: int32 [16, 8, 4], P('gx', 'gy'), may hold values from 0 to 7, as said below
Outputs:
- purified: float32 [16, 8, 8, 64, 1024], P('gx', 'gy')
- occupation: float32 [4], replicated
Inputs may be any that keep to these rules, and one draw needn't show every extreme that they name: moves is a permutation of the 1024 row ids. Rows leave in 8 waves: in each wave every brick sends one row to the brick beside it (periodic, among the eight around it) in that wave's direction, the waves' directions all differ, and the row lands in the slot that the receiving brick emptied in the same wave; all other rows keep their id. cols[i, j, r, 0] is r; the 16 entries of a row are distinct. `halo_rows`: the 4 entries of a brick are distinct.
All inputs are finite; a program needn't handle non-finite values.
Results may differ from a plain program's by a relative error of at most 0.0003.
Values sent between devices are 32-bit elements; how exact they have to be, the bound alone decides.
A program may use at most 192 MiB of HBM per device.

v0:
```python
import jax
import jax.numpy as jnp
import numpy as np
from jax import lax
from jax.sharding import PartitionSpec as P

WAVES = 8
STEPS = 2


step_x = np.array([-1, -1, -1, 0, 0, 1, 1, 1])
step_y = np.array([-1, 0, 1, -1, 1, -1, 0, 1])
highest = lax.Precision.HIGHEST


def extended_2(block, sides, width):
    for axis, dim in sides:
        count = lax.axis_size(axis)
        forward = [(i, i + 1) for i in range(count - 1)]
        forward.append((count - 1, 0))
        backward = [(target, source) for source, target in forward]
        low = lax.ppermute(
            lax.slice_in_dim(block, block.shape[dim] - width, None, axis=dim), axis, forward
        )
        high = lax.ppermute(lax.slice_in_dim(block, 0, width, axis=dim), axis, backward)
        block = jnp.concatenate([low, block, high], axis=dim)
    return block


def neighbour_rows(extended):
    inner = extended.shape[2:]
    nine = extended.reshape((9,) + inner)
    picked = jnp.concatenate([nine[:4], nine[5:]], 0)
    return picked.reshape((8 * inner[0],) + inner[1:])


def slot_trace(current):
    block = current.shape[1]
    return jnp.sum(jnp.diagonal(current[:, :, :block], axis1=1, axis2=2))


def square_rows(current, local_cols, own_ids, candidates, candidate_ids):
    row_count, block, strip = current.shape
    slots = local_cols.shape[1]
    group = min(4, row_count)

    def one_group(pieces):
        mine, my_cols, my_ids = pieces
        width = mine.shape[0]
        far = jnp.take(candidates, my_cols, axis=0)
        far_ids = jnp.take(candidate_ids, my_cols, axis=0)
        match = far_ids[:, :, :, None] == my_ids[:, None, None, :]
        picked = jnp.argmax(match.astype(jnp.int32), axis=2)
        found = jnp.any(match, axis=2)
        far_blocks = far.reshape(width, slots, block, slots, block)
        aligned = jnp.take_along_axis(far_blocks, picked[:, :, None, :, None], axis=3)
        aligned = jnp.where(found[:, :, None, :, None], aligned, 0.0).reshape(
            width, slots, block, strip
        )
        return jnp.einsum("gatb,gtbx->gax", mine, aligned, precision=highest)

    grouped = (
        current.reshape(row_count // group, group, block, slots, block),
        local_cols.reshape(row_count // group, group, slots),
        own_ids.reshape(row_count // group, group, slots),
    )
    return lax.map(one_group, grouped).reshape(row_count, block, strip)


def shards(density, moves, cols, halo_rows):
    row_count = density.shape[2]
    block = density.shape[3]
    strip = density.shape[4]
    slots = cols.shape[3]
    rim_count = halo_rows.shape[2]
    count_x = lax.axis_size("gx")
    count_y = lax.axis_size("gy")
    index_x = lax.axis_index("gx")
    index_y = lax.axis_index("gy")
    myself = index_x * count_y + index_y
    offsets_x = jnp.asarray(step_x, dtype=jnp.int32)
    offsets_y = jnp.asarray(step_y, dtype=jnp.int32)
    neighbours = (index_x + offsets_x) % count_x * count_y + (index_y + offsets_y) % count_y
    previous = density.reshape(row_count, block * strip)
    target = moves.reshape(row_count)
    dest_dev = target // row_count
    dest_slot = target % row_count
    leaving = dest_dev != myself
    slot_ids = jnp.arange(row_count, dtype=jnp.int32)
    labels = (target + 1).astype(jnp.float32)
    rank = jnp.cumsum(leaving.astype(jnp.int32)) - 1
    waves = jnp.arange(WAVES, dtype=jnp.int32)
    chosen = (leaving[None, :] & (rank[None, :] == waves[:, None])).astype(jnp.float32)
    outgoing = jnp.dot(chosen, previous, precision=highest).reshape(1, 1, WAVES, block * strip)
    outgoing_marks = jnp.dot(chosen, labels, precision=highest).reshape(1, 1, WAVES)
    extended, extended_marks = (
        extended_2(outgoing, (("gx", 0), ("gy", 1)), 1),
        extended_2(outgoing_marks, (("gx", 0), ("gy", 1)), 1),
    )
    arrived = extended.reshape(9 * WAVES, block * strip)
    arrived_marks = extended_marks.reshape(9 * WAVES)
    wanted = (myself * row_count + slot_ids + 1).astype(jnp.float32)
    keep = ((~leaving)[None, :] & (dest_slot[None, :] == slot_ids[:, None])).astype(jnp.float32)
    take_in = (arrived_marks[None, :] == wanted[:, None]).astype(jnp.float32)
    current = jnp.dot(
        jnp.concatenate([keep, take_in], 1),
        jnp.concatenate([previous, arrived], 0),
        precision=highest,
    ).reshape(row_count, block, strip)
    local_cols = cols.reshape(row_count, slots)
    own_rims = halo_rows.reshape(rim_count)
    near_lists = neighbour_rows(extended_2(halo_rows, (("gx", 0), ("gy", 1)), 1))
    near_firsts = jnp.repeat(neighbours * row_count, rim_count)
    table = jnp.concatenate([myself * row_count + slot_ids, near_firsts + near_lists])
    pool = table.shape[0]
    own_ids = jnp.sum(
        jnp.where(local_cols[:, :, None] == jnp.arange(pool, dtype=jnp.int32), table, 0), axis=2
    )
    rim_ids = jnp.take(own_ids, own_rims, axis=0).reshape(1, 1, rim_count, slots)
    near_ids = neighbour_rows(extended_2(rim_ids, (("gx", 0), ("gy", 1)), 1))
    candidate_ids = jnp.concatenate([own_ids, near_ids], 0)
    scale = 1.0 / (count_x * count_y * row_count * block)
    results = []
    for step in range(STEPS):
        rims = jnp.take(current, own_rims, axis=0).reshape(1, 1, rim_count, block, strip)
        near_strips = neighbour_rows(extended_2(rims, (("gx", 0), ("gy", 1)), 1))
        candidates = jnp.concatenate([current, near_strips], 0)
        squared = square_rows(current, local_cols, own_ids, candidates, candidate_ids)
        pair = jnp.stack([slot_trace(current), slot_trace(squared)]) * scale
        results.append(lax.psum(pair, ("gx", "gy")))
        if step % 2 == 1:
            current = 2.0 * current - squared
        else:
            current = squared
    occupation = jnp.concatenate(results)
    return (current.reshape(density.shape), occupation)


def solution(mesh):
    in_specs = (
        P("gx", "gy", None, None, None),
        P("gx", "gy", None),
        P("gx", "gy", None, None),
        P("gx", "gy", None),
    )
    out_specs = (P("gx", "gy", None, None, None), P())
    return jax.shard_map(shards, mesh=mesh, in_specs=in_specs, out_specs=out_specs, check_vma=False)
```

profile of v0, /device:TPU:1, one launch (start us, length us, event | category | flops | bytes accessed | tf_op | source)
XLA Modules:
  0.0 1284.0 jit_solution(11348066024362569463)
XLA Ops:
  14.2 44.3 %collective-permute-done.5 = f32[1,1,8,65536]{3,2,1,0:T(8,128)S(1)} collective-permute-done((f32[1,1,8,65536]{3,2,1,0:T(8,128)S(1)}, f32[1,1,8,65536]{3,2,1,0:T(8,128)S(1)}, u32[]{:S(2)}, u32[]{:S(2)}) %collective-permute-start.5) | collective-permute-done | bytes 2097184 | tf_op jit(solution)/shard_map/ppermute | solution.py:25
  79.3 60.0 %collective-permute-done.3 = f32[3,1,8]{2,1,0:T(1,128)S(1)} collective-permute-done((f32[3,1,8]{2,1,0:T(1,128)S(1)}, f32[3,1,8]{2,1,0:T(1,128)S(1)}, u32[]{:S(2)}, u32[]{:S(2)}) %collective-permute-start.3) | collective-permute-done | bytes 128 | tf_op jit(solution)/shard_map/ppermute | solution.py:25
  163.8 20.5 %collective-permute-done.17 = f32[1,1,4,64,1024]{4,3,2,1,0:T(8,128)S(1)} collective-permute-done((f32[1,1,4,64,1024]{4,3,2,1,0:T(8,128)S(1)}, f32[1,1,4,64,1024]{4,3,2,1,0:T(8,128)S(1)}, u32[]{:S(2)}, u32[]{:S(2)}) %collective-permute-start.17) | collective-permute-done | bytes 1048608 | tf_op jit(solution)/shard_map/ppermute | solution.py:25
  204.7 26.6 %collective-permute-done.11 = s32[3,1,4]{2,1,0:T(1,128)S(1)} collective-permute-done((s32[3,1,4]{2,1,0:T(1,128)S(1)}, s32[3,1,4]{2,1,0:T(1,128)S(1)}, u32[]{:S(2)}, u32[]{:S(2)}) %collective-permute-start.11) | collective-permute-done | bytes 80 | tf_op jit(solution)/shard_map/ppermute | solution.py:25
  270.6 422.9 %while.20 = (s32[]{:T(128)}, f32[2,4,64,1024]{3,2,1,0:T(8,128)}, f32[2,4,64,16,64]{4,3,2,1,0:T(8,128)}, s32[2,4,16]{2,1,0:T(4,128)S(1)}, s32[40,16]{1,0:T(8,128)...) while((s32[]{:T(128)}, f32[2,4,64,1024]{3,2,1,0:T(8,128)}, ...), condition=%wide.region_5.10_spmd, body=%wide.region_2.9_spmd.sunk | while | flops 3234000384 | bytes 289483808 | solution.py:67
  299.8 25.8 %reshape.567 = f32[4,16,64,16,64]{4,3,2,1,0:T(8,128)} reshape(f32[4,16,64,1024]{3,2,1,0:T(8,128)} %broadcast_select_fusion.8) | data formatting | bytes 33554432 | tf_op jit(solution)/shard_map/while/body/eval_jaxpr/reshape | solution.py:55
  325.6 30.5 %copy.122 = f32[4,16,64,16,64]{4,2,3,1,0:T(8,128)} copy(f32[4,16,64,16,64]{4,3,2,1,0:T(8,128)} %reshape.567) | data formatting | bytes 33554432 | tf_op jit(solution)/shard_map/while/body/eval_jaxpr/reshape | solution.py:55
  356.1 43.1 %gather_fusion.2 = f32[1024,64,64]{2,1,0:T(8,128)} fusion(f32[4,16,64,16,64]{4,2,3,1,0:T(8,128)} %copy.122, s32[1024]{0:T(1024)S(1)} %reshape.568), kind=kCustom, calls=%fused_computation.3.clone.clone.1 | custom fusion | bytes 33566720 | tf_op jit(solution)/shard_map/while/body/eval_jaxpr/jit(take_along_axis)/gather | solution.py:56
  412.1 25.5 %copy.123 = f32[4,16,64,16,64]{4,3,2,1,0:T(8,128)} copy(f32[4,16,64,16,64]{4,2,3,1,0:T(8,128)S(1)} %bitcast_select_fusion.5) | data formatting | bytes 33554432 | tf_op jit(solution)/shard_map/while/body/eval_jaxpr/jit(_where)/select_n | solution.py:57
  437.6 28.3 %reshape.569 = f32[4,16,64,1024]{3,2,1,0:T(8,128)} reshape(f32[4,16,64,16,64]{4,3,2,1,0:T(8,128)} %copy.123) | data formatting | bytes 33554432 | tf_op jit(solution)/shard_map/while/body/eval_jaxpr/reshape | solution.py:57
  465.8 16.2 %fusion.54 = f32[2,4,64,1024]{3,2,1,0:T(8,128)} fusion(f32[2,4,64,1024]{3,2,1,0:T(8,128)} %get-tuple-element.314, s32[]{:T(128)S(6)} %copy.133, f32[4,16,64,1024]{3,2,1,0:T(8,128)} %reshape.569, f32[1,4,64,16,64]{4,3,2,1,0:T(8,128)S(1)} %constant_dynamic-slice_fusion.4), kind=kOutput, calls=%fused_computation.17.clone.1 | convolution fusion | flops 3221225472 | bytes 18874372 | tf_op jit(solution)/shard_map/while/body/eval_jaxpr/gatb,gtbx->gax/dot_general | solution.py:60
  511.2 25.8 %reshape.567 = f32[4,16,64,16,64]{4,3,2,1,0:T(8,128)} reshape(f32[4,16,64,1024]{3,2,1,0:T(8,128)} %broadcast_select_fusion.8) | data formatting | bytes 33554432 | tf_op jit(solution)/shard_map/while/body/eval_jaxpr/reshape | solution.py:55
  537.0 30.5 %copy.122 = f32[4,16,64,16,64]{4,2,3,1,0:T(8,128)} copy(f32[4,16,64,16,64]{4,3,2,1,0:T(8,128)} %reshape.567) | data formatting | bytes 33554432 | tf_op jit(solution)/shard_map/while/body/eval_jaxpr/reshape | solution.py:55
  567.6 43.0 %gather_fusion.2 = f32[1024,64,64]{2,1,0:T(8,128)} fusion(f32[4,16,64,16,64]{4,2,3,1,0:T(8,128)} %copy.122, s32[1024]{0:T(1024)S(1)} %reshape.568), kind=kCustom, calls=%fused_computation.3.clone.clone.1 | custom fusion | bytes 33566720 | tf_op jit(solution)/shard_map/while/body/eval_jaxpr/jit(take_along_axis)/gather | solution.py:56
  623.4 25.5 %copy.123 = f32[4,16,64,16,64]{4,3,2,1,0:T(8,128)} copy(f32[4,16,64,16,64]{4,2,3,1,0:T(8,128)S(1)} %bitcast_select_fusion.5) | data formatting | bytes 33554432 | tf_op jit(solution)/shard_map/while/body/eval_jaxpr/jit(_where)/select_n | solution.py:57
  648.8 28.3 %reshape.569 = f32[4,16,64,1024]{3,2,1,0:T(8,128)} reshape(f32[4,16,64,16,64]{4,3,2,1,0:T(8,128)} %copy.123) | data formatting | bytes 33554432 | tf_op jit(solution)/shard_map/while/body/eval_jaxpr/reshape | solution.py:57
  699.9 19.6 %collective-permute-done.21 = f32[1,1,4,64,1024]{4,3,2,1,0:T(8,128)S(1)} collective-permute-done((f32[1,1,4,64,1024]{4,3,2,1,0:T(8,128)S(1)}, f32[1,1,4,64,1024]{4,3,2,1,0:T(8,128)S(1)}, u32[]{:S(2)}, u32[]{:S(2)}) %collective-permute-start.21) | collective-permute-done | bytes 1048608 | tf_op jit(solution)/shard_map/ppermute | solution.py:25
  741.5 22.9 %collective-permute-done.23 = f32[3,1,4,64,1024]{4,3,2,1,0:T(8,128)} collective-permute-done((f32[3,1,4,64,1024]{4,3,2,1,0:T(8,128)}, f32[3,1,4,64,1024]{4,3,2,1,0:T(8,128)}, u32[]{:S(2)}, u32[]{:S(2)}) %collective-permute-start.23) | collective-permute-done | bytes 3145760 | tf_op jit(solution)/shard_map/ppermute | solution.py:25
  784.9 423.2 %while.21 = (s32[]{:T(128)}, f32[2,4,64,1024]{3,2,1,0:T(8,128)}, f32[2,4,64,16,64]{4,3,2,1,0:T(8,128)}, s32[2,4,16]{2,1,0:T(4,128)S(1)}, s32[40,16]{1,0:T(8,128)...) while((s32[]{:T(128)}, f32[2,4,64,1024]{3,2,1,0:T(8,128)}, ...), condition=%wide.region_9.14_spmd, body=%wide.region_6.13_spmd.sunk | while | flops 3234000384 | bytes 289483808 | solution.py:67
  814.4 25.8 %reshape.577 = f32[4,16,64,16,64]{4,3,2,1,0:T(8,128)} reshape(f32[4,16,64,1024]{3,2,1,0:T(8,128)} %broadcast_select_fusion.10) | data formatting | bytes 33554432 | tf_op jit(solution)/shard_map/while/body/eval_jaxpr/reshape | solution.py:55
  840.2 30.5 %copy.125 = f32[4,16,64,16,64]{4,2,3,1,0:T(8,128)} copy(f32[4,16,64,16,64]{4,3,2,1,0:T(8,128)} %reshape.577) | data formatting | bytes 33554432 | tf_op jit(solution)/shard_map/while/body/eval_jaxpr/reshape | solution.py:55
  870.7 43.1 %gather_fusion.5 = f32[1024,64,64]{2,1,0:T(8,128)} fusion(f32[4,16,64,16,64]{4,2,3,1,0:T(8,128)} %copy.125, s32[1024]{0:T(1024)S(1)} %reshape.578), kind=kCustom, calls=%fused_computation.7.clone.clone.1 | custom fusion | bytes 33566720 | tf_op jit(solution)/shard_map/while/body/eval_jaxpr/jit(take_along_axis)/gather | solution.py:56
  926.7 25.5 %copy.126 = f32[4,16,64,16,64]{4,3,2,1,0:T(8,128)} copy(f32[4,16,64,16,64]{4,2,3,1,0:T(8,128)S(1)} %bitcast_select_fusion.6) | data formatting | bytes 33554432 | tf_op jit(solution)/shard_map/while/body/eval_jaxpr/jit(_where)/select_n | solution.py:57
  952.1 28.3 %reshape.579 = f32[4,16,64,1024]{3,2,1,0:T(8,128)} reshape(f32[4,16,64,16,64]{4,3,2,1,0:T(8,128)} %copy.126) | data formatting | bytes 33554432 | tf_op jit(solution)/shard_map/while/body/eval_jaxpr/reshape | solution.py:57
  980.4 16.2 %fusion.57 = f32[2,4,64,1024]{3,2,1,0:T(8,128)} fusion(f32[2,4,64,1024]{3,2,1,0:T(8,128)} %get-tuple-element.338, s32[]{:T(128)S(6)} %copy.139, f32[4,16,64,1024]{3,2,1,0:T(8,128)} %reshape.579, f32[1,4,64,16,64]{4,3,2,1,0:T(8,128)S(1)} %constant_dynamic-slice_fusion.5), kind=kOutput, calls=%fused_computation.35.clone.1 | convolution fusion | flops 3221225472 | bytes 18874372 | tf_op jit(solution)/shard_map/while/body/eval_jaxpr/gatb,gtbx->gax/dot_general | solution.py:60
  1025.8 25.8 %reshape.577 = f32[4,16,64,16,64]{4,3,2,1,0:T(8,128)} reshape(f32[4,16,64,1024]{3,2,1,0:T(8,128)} %broadcast_select_fusion.10) | data formatting | bytes 33554432 | tf_op jit(solution)/shard_map/while/body/eval_jaxpr/reshape | solution.py:55
  1051.6 30.5 %copy.125 = f32[4,16,64,16,64]{4,2,3,1,0:T(8,128)} copy(f32[4,16,64,16,64]{4,3,2,1,0:T(8,128)} %reshape.577) | data formatting | bytes 33554432 | tf_op jit(solution)/shard_map/while/body/eval_jaxpr/reshape | solution.py:55
  1082.2 43.0 %gather_fusion.5 = f32[1024,64,64]{2,1,0:T(8,128)} fusion(f32[4,16,64,16,64]{4,2,3,1,0:T(8,128)} %copy.125, s32[1024]{0:T(1024)S(1)} %reshape.578), kind=kCustom, calls=%fused_computation.7.clone.clone.1 | custom fusion | bytes 33566720 | tf_op jit(solution)/shard_map/while/body/eval_jaxpr/jit(take_along_axis)/gather | solution.py:56
  1138.0 25.5 %copy.126 = f32[4,16,64,16,64]{4,3,2,1,0:T(8,128)} copy(f32[4,16,64,16,64]{4,2,3,1,0:T(8,128)S(1)} %bitcast_select_fusion.6) | data formatting | bytes 33554432 | tf_op jit(solution)/shard_map/while/body/eval_jaxpr/jit(_where)/select_n | solution.py:57
  1163.4 28.3 %reshape.579 = f32[4,16,64,1024]{3,2,1,0:T(8,128)} reshape(f32[4,16,64,16,64]{4,3,2,1,0:T(8,128)} %copy.126) | data formatting | bytes 33554432 | tf_op jit(solution)/shard_map/while/body/eval_jaxpr/reshape | solution.py:57
  1191.7 16.2 %fusion.57 = f32[2,4,64,1024]{3,2,1,0:T(8,128)} fusion(f32[2,4,64,1024]{3,2,1,0:T(8,128)} %get-tuple-element.338, s32[]{:T(128)S(6)} %copy.139, f32[4,16,64,1024]{3,2,1,0:T(8,128)} %reshape.579, f32[1,4,64,16,64]{4,3,2,1,0:T(8,128)S(1)} %constant_dynamic-slice_fusion.5), kind=kOutput, calls=%fused_computation.35.clone.1 | convolution fusion | flops 3221225472 | bytes 18874372 | tf_op jit(solution)/shard_map/while/body/eval_jaxpr/gatb,gtbx->gax/dot_general | solution.py:60
  1217.4 65.7 %all-reduce = (f32[2]{0:T(128)S(1)}, f32[2]{0:T(128)S(1)}) all-reduce(f32[2]{0:T(128)S(1)} %get-tuple-element.206, f32[2]{0:T(128)S(1)} %get-tuple-element.205), channel_id=1, replica_groups=mesh['gx'=16,'gy'=8] {'gx','gy'}, use_global_device_ids=true, to_apply=%region_14.19 | all-reduce | flops 4 | bytes 32 | tf_op jit(solution)/shard_map/psum | solution.py:130
  (225 shorter events, 361.2 us)
Async XLA Ops:
  6.3 63.7 %copy-start.18 = (s32[1,1,8]{2,1,0:T(1,128)S(1)}, s32[1,1,8]{2,1,0:T(1,128)}, u32[]{:S(2)}) copy-start(s32[1,1,8]{2,1,0:T(1,128)} %param.19) | copy-start | bytes 100
  6.3 65.5 %copy-start.19 = (s32[1,1,4]{2,1,0:T(1,128)S(1)}, s32[1,1,4]{2,1,0:T(1,128)}, u32[]{:S(2)}) copy-start(s32[1,1,4]{2,1,0:T(1,128)} %param.21) | copy-start | bytes 52
  7.4 51.1 %collective-permute-start.5 = (f32[1,1,8,65536]{3,2,1,0:T(8,128)S(1)}, f32[1,1,8,65536]{3,2,1,0:T(8,128)S(1)}, u32[]{:S(2)}, u32[]{:S(2)}) collective-permute-start(f32[1,1,8,65536]{3,2,1,0:T(8,128)S(1)} %convolution_bitcast_fusion), channel_id=1, source_target_pairs={{8,0},{16,8},{24,16},{32,24},{40,32},{48,40},{56,48},{64,56},{72,6... | collective-permute-start | bytes 6291464 | tf_op jit(solution)/shard_map/ppermute | solution.py:25
  14.2 49.5 %collective-permute-start.4 = (f32[1,1,8,65536]{3,2,1,0:T(8,128)S(1)}, f32[1,1,8,65536]{3,2,1,0:T(8,128)S(1)}, u32[]{:S(2)}, u32[]{:S(2)}) collective-permute-start(f32[1,1,8,65536]{3,2,1,0:T(8,128)S(1)} %convolution_bitcast_fusion), channel_id=1, source_target_pairs={{0,8},{8,16},{16,24},{24,32},{32,40},{40,48},{48,56},{56,64},{64,7... | collective-permute-start | bytes 6291464 | tf_op jit(solution)/shard_map/ppermute | solution.py:22
  67.0 72.5 %collective-permute-start.7 = (f32[3,1,8,65536]{3,2,1,0:T(8,128)}, f32[3,1,8,65536]{3,2,1,0:T(8,128)}, u32[]{:S(2)}, u32[]{:S(2)}) collective-permute-start(f32[3,1,8,65536]{3,2,1,0:T(8,128)} %pad_maximum_fusion.7), channel_id=1, source_target_pairs={{1,0},{2,1},{3,2},{4,3},{5,4},{6,5},{7,6},{0,7},{9,8},{10,9},{11,1... | collective-permute-start | bytes 18874376 | tf_op jit(solution)/shard_map/ppermute | solution.py:25
  68.8 70.7 %collective-permute-start.6 = (f32[3,1,8,65536]{3,2,1,0:T(8,128)}, f32[3,1,8,65536]{3,2,1,0:T(8,128)}, u32[]{:S(2)}, u32[]{:S(2)}) collective-permute-start(f32[3,1,8,65536]{3,2,1,0:T(8,128)} %pad_maximum_fusion.7), channel_id=1, source_target_pairs={{0,1},{1,2},{2,3},{3,4},{4,5},{5,6},{6,7},{7,0},{8,9},{9,10},{10,1... | collective-permute-start | bytes 18874376 | tf_op jit(solution)/shard_map/ppermute | solution.py:22
  70.1 2.4 collective-permute-start.1
  71.5 5.9 collective-permute-start
  71.8 85.9 %copy-start.13 = (s32[1024]{0:T(1024)}, s32[1024]{0:T(1024)S(1)}, u32[]{:S(2)}) copy-start(s32[1024]{0:T(1024)S(1)} %pad_clamp_fusion.2) | copy-start | bytes 12292
  71.8 160.9 %copy-start.14 = (pred[4]{0:T(512)(128)(4,1)}, pred[4]{0:T(512)(128)(4,1)S(1)}, u32[]{:S(2)}) copy-start(pred[4]{0:T(512)(128)(4,1)S(1)} %compare_and_fusion.2) | copy-start | bytes 16
  77.3 62.0 %collective-permute-start.3 = (f32[3,1,8]{2,1,0:T(1,128)S(1)}, f32[3,1,8]{2,1,0:T(1,128)S(1)}, u32[]{:S(2)}, u32[]{:S(2)}) collective-permute-start(f32[3,1,8]{2,1,0:T(1,128)S(1)} %pad_maximum_fusion.11), channel_id=1, source_target_pairs={{1,0},{2,1},{3,2},{4,3},{5,4},{6,5},{7,6},{0,7},{9,8},{10,9},{11,1... | collective-permute-start | bytes 296 | tf_op jit(solution)/shard_map/ppermute | solution.py:25
  79.2 60.1 %collective-permute-start.2 = (f32[3,1,8]{2,1,0:T(1,128)S(1)}, f32[3,1,8]{2,1,0:T(1,128)S(1)}, u32[]{:S(2)}, u32[]{:S(2)}) collective-permute-start(f32[3,1,8]{2,1,0:T(1,128)S(1)} %pad_maximum_fusion.11), channel_id=1, source_target_pairs={{0,1},{1,2},{2,3},{3,4},{4,5},{5,6},{6,7},{7,0},{8,9},{9,10},{10,1... | collective-permute-start | bytes 296 | tf_op jit(solution)/shard_map/ppermute | solution.py:22
  155.1 94.9 %copy-start.1 = (f32[8,65536]{1,0:T(8,128)}, f32[8,65536]{1,0:T(8,128)S(1)}, u32[]{:S(2)}) copy-start(f32[8,65536]{1,0:T(8,128)S(1)} %fusion.8) | copy-start | bytes 6291460
  155.2 42.0 %copy-start.16 = (s32[8]{0:T(128)S(1)}, s32[8]{0:T(128)}, u32[]{:S(2)}) copy-start(s32[8]{0:T(128)} %constant.173.clone) | copy-start | bytes 100
  155.2 76.7 %copy-start.12 = (s32[1,1,8,16]{3,2,1,0:T(8,128)S(1)}, s32[1,1,8,16]{3,2,1,0:T(8,128)}, u32[]{:S(2)}) copy-start(s32[1,1,8,16]{3,2,1,0:T(8,128)} %param.20) | copy-start | bytes 1540
  162.3 22.0 %collective-permute-start.17 = (f32[1,1,4,64,1024]{4,3,2,1,0:T(8,128)S(1)}, f32[1,1,4,64,1024]{4,3,2,1,0:T(8,128)S(1)}, u32[]{:S(2)}, u32[]{:S(2)}) collective-permute-start(f32[1,1,4,64,1024]{4,3,2,1,0:T(8,128)S(1)} %select_bitcast_fusion.1), channel_id=1, source_target_pairs={{8,0},{16,8},{24,16},{32,24},{40,32},{48,40},{56,48},{64,56},{72,6... | collective-permute-start | bytes 3145736 | tf_op jit(solution)/shard_map/ppermute | solution.py:25
  163.7 24.6 %collective-permute-start.16 = (f32[1,1,4,64,1024]{4,3,2,1,0:T(8,128)S(1)}, f32[1,1,4,64,1024]{4,3,2,1,0:T(8,128)S(1)}, u32[]{:S(2)}, u32[]{:S(2)}) collective-permute-start(f32[1,1,4,64,1024]{4,3,2,1,0:T(8,128)S(1)} %select_bitcast_fusion.1), channel_id=1, source_target_pairs={{0,8},{8,16},{16,24},{24,32},{32,40},{40,48},{48,56},{56,64},{64,7... | collective-permute-start | bytes 3145736 | tf_op jit(solution)/shard_map/ppermute | solution.py:22
  190.4 59.6 %collective-permute-start.19 = (f32[3,1,4,64,1024]{4,3,2,1,0:T(8,128)}, f32[3,1,4,64,1024]{4,3,2,1,0:T(8,128)}, u32[]{:S(2)}, u32[]{:S(2)}) collective-permute-start(f32[3,1,4,64,1024]{4,3,2,1,0:T(8,128)} %pad_maximum_fusion.8), channel_id=1, source_target_pairs={{1,0},{2,1},{3,2},{4,3},{5,4},{6,5},{7,6},{0,7},{9,8},{10,9},{11,1... | collective-permute-start | bytes 9437192 | tf_op jit(solution)/shard_map/ppermute | solution.py:25
  194.7 55.4 %collective-permute-start.18 = (f32[3,1,4,64,1024]{4,3,2,1,0:T(8,128)}, f32[3,1,4,64,1024]{4,3,2,1,0:T(8,128)}, u32[]{:S(2)}, u32[]{:S(2)}) collective-permute-start(f32[3,1,4,64,1024]{4,3,2,1,0:T(8,128)} %pad_maximum_fusion.8), channel_id=1, source_target_pairs={{0,1},{1,2},{2,3},{3,4},{4,5},{5,6},{6,7},{7,0},{8,9},{9,10},{10,1... | collective-permute-start | bytes 9437192 | tf_op jit(solution)/shard_map/ppermute | solution.py:22
  195.7 6.7 collective-permute-start.9
  196.7 5.7 collective-permute-start.8
  202.4 28.9 %collective-permute-start.11 = (s32[3,1,4]{2,1,0:T(1,128)S(1)}, s32[3,1,4]{2,1,0:T(1,128)S(1)}, u32[]{:S(2)}, u32[]{:S(2)}) collective-permute-start(s32[3,1,4]{2,1,0:T(1,128)S(1)} %constant_dynamic-update-slice_fusion), channel_id=1, source_target_pairs={{1,0},{2,1},{3,2},{4,3},{5,4},{6,5},{7,6},{0,7},{9,8},{10,9},{11,1... | collective-permute-start | bytes 152 | tf_op jit(solution)/shard_map/ppermute | solution.py:25
  204.7 26.6 %collective-permute-start.10 = (s32[3,1,4]{2,1,0:T(1,128)S(1)}, s32[3,1,4]{2,1,0:T(1,128)S(1)}, u32[]{:S(2)}, u32[]{:S(2)}) collective-permute-start(s32[3,1,4]{2,1,0:T(1,128)S(1)} %constant_dynamic-update-slice_fusion), channel_id=1, source_target_pairs={{0,1},{1,2},{2,3},{3,4},{4,5},{5,6},{6,7},{7,0},{8,9},{9,10},{10,1... | collective-permute-start | bytes 152 | tf_op jit(solution)/shard_map/ppermute | solution.py:22
  232.8 2.4 collective-permute-start.13
  233.7 6.1 collective-permute-start.12
  239.9 5.7 collective-permute-start.15
  244.8 1.2 collective-permute-start.14
  270.6 426.3 %copy-start.15 = (pred[4]{0:T(512)(128)(4,1)S(1)}, pred[4]{0:T(512)(128)(4,1)}, u32[]{:S(2)}) copy-start(pred[4]{0:T(512)(128)(4,1)} %copy-done.14) | copy-start | bytes 16
  698.4 21.1 %collective-permute-start.21 = (f32[1,1,4,64,1024]{4,3,2,1,0:T(8,128)S(1)}, f32[1,1,4,64,1024]{4,3,2,1,0:T(8,128)S(1)}, u32[]{:S(2)}, u32[]{:S(2)}) collective-permute-start(f32[1,1,4,64,1024]{4,3,2,1,0:T(8,128)S(1)} %select_bitcast_fusion), channel_id=1, source_target_pairs={{8,0},{16,8},{24,16},{32,24},{40,32},{48,40},{56,48},{64,56},{72,6... | collective-permute-start | bytes 3145736 | tf_op jit(solution)/shard_map/ppermute | solution.py:25
  698.7 24.3 %collective-permute-start.20 = (f32[1,1,4,64,1024]{4,3,2,1,0:T(8,128)S(1)}, f32[1,1,4,64,1024]{4,3,2,1,0:T(8,128)S(1)}, u32[]{:S(2)}, u32[]{:S(2)}) collective-permute-start(f32[1,1,4,64,1024]{4,3,2,1,0:T(8,128)S(1)} %select_bitcast_fusion), channel_id=1, source_target_pairs={{0,8},{8,16},{16,24},{24,32},{32,40},{40,48},{48,56},{56,64},{64,7... | collective-permute-start | bytes 3145736 | tf_op jit(solution)/shard_map/ppermute | solution.py:22
  725.1 39.4 %collective-permute-start.23 = (f32[3,1,4,64,1024]{4,3,2,1,0:T(8,128)}, f32[3,1,4,64,1024]{4,3,2,1,0:T(8,128)}, u32[]{:S(2)}, u32[]{:S(2)}) collective-permute-start(f32[3,1,4,64,1024]{4,3,2,1,0:T(8,128)} %pad_maximum_fusion.9), channel_id=1, source_target_pairs={{1,0},{2,1},{3,2},{4,3},{5,4},{6,5},{7,6},{0,7},{9,8},{10,9},{11,1... | collective-permute-start | bytes 9437192 | tf_op jit(solution)/shard_map/ppermute | solution.py:25
  729.6 34.8 %collective-permute-start.22 = (f32[3,1,4,64,1024]{4,3,2,1,0:T(8,128)}, f32[3,1,4,64,1024]{4,3,2,1,0:T(8,128)}, u32[]{:S(2)}, u32[]{:S(2)}) collective-permute-start(f32[3,1,4,64,1024]{4,3,2,1,0:T(8,128)} %pad_maximum_fusion.9), channel_id=1, source_target_pairs={{0,1},{1,2},{2,3},{3,4},{4,5},{5,6},{6,7},{7,0},{8,9},{9,10},{10,1... | collective-permute-start | bytes 9437192 | tf_op jit(solution)/shard_map/ppermute | solution.py:22
  (12 other events, 164.4 us)
where the time goes:
time: 1300 us; the launch traced here: 1280 us
  local copies, waits for them, and re-layouts  712 us (55%)
  waiting for transfers between devices  224 us (17%)
  other arithmetic  169 us (13%)
  matrix products  74.5 us (6%)
  blocking collectives  65.7 us (5%)
  starting transfers between devices  37 us (3%)
    reshape x8, local copies, waits for them, and re-layouts, one_group(): far_blocks = far.reshape(width, slots, block, slots, block)  225 us
    ppermute x12, waiting for transfers between devices, extended_2(): lax.ppermute(lax.slice_in_dim(block, 0, width, axis=dim), axis, backward)  196 us
    gather x8, local copies, waits for them, and re-layouts, one_group(): jnp.take_along_axis(far_blocks, picked[:, :, None, :, None], axis=3)  173 us
    reshape x4, local copies, waits for them, and re-layouts, one_group(): jnp.where(found[:, :, None, :, None], aligned, 0.0)  113 us
    select_n x4, local copies, waits for them, and re-layouts, one_group(): jnp.where(found[:, :, None, :, None], aligned, 0.0)  102 us
    psum x1, blocking collectives, shards(): results.append(lax.psum(pair, ('gx', 'gy')))  65.7 us
    dot_general x4, matrix products, one_group(): return jnp.einsum('gatb,gtbx->gax', mine, aligned, precision=highest)  64.8 us
    gather x4, local copies, waits for them, and re-layouts, one_group(): far = jnp.take(candidates, my_cols, axis=0)  51.3 us
  transfers between devices with their start and end apart: 24, of which 16 were waited for; matrix products, arithmetic and copies ran while one was open for 1% of the time, Pallas kernels for 0%

commit v1 on v0

v1 whole, which is shorter than its diff:
```python
import functools

import jax
import jax.numpy as jnp
from jax import lax
from jax.experimental import pallas as pl
from jax.experimental.pallas import tpu as pltpu
from jax.sharding import PartitionSpec as P

MESH = pl.DeviceIdType.MESH
f32 = jnp.float32
bf16 = jnp.bfloat16
i32 = jnp.int32

DIRS = ((-1, -1), (-1, 0), (-1, 1), (0, -1), (0, 1), (1, -1), (1, 0), (1, 1))

ROWS = 8
SLOTS = 16
BLOCK = 64
HALO = 4
STRIP = SLOTS * BLOCK
PAIRS = SLOTS // 2
POOL = ROWS + 8 * HALO

I, Y, ZM, ZP, ZMI, ZPI, ZMY, ZPY = range(8)


def kernel(nx, ny, moves_s, rims_s, meta, dens_hbm, out_hbm, occ_s,
           dens, stage, mig, cur, halo, near, left, prod, acc, outbuf,
           info, infos, tab, tab_s, role_s, parts, sum_y, sum_x,
           local_sem, tab_sem, out_sem, mig_send, mig_recv, info_send, info_recv,
           halo_send, halo_recv, sumy_send, sumy_recv, sumx_send, sumx_recv):
    ix = lax.axis_index("gx")
    iy = lax.axis_index("gy")
    me = ix * ny + iy
    cross = 2 * lax.rem(iy, 2) - 1
    inner = -cross

    def at(dx, dy):
        return (lax.rem(ix + dx + nx, nx), lax.rem(iy + dy + ny, ny))

    load = pltpu.make_async_copy(dens_hbm.at[0, 0], dens, local_sem)
    load.start()

    barrier = pltpu.get_barrier_semaphore()
    greeted = [at(dx, dy) for dx, dy in DIRS if dx and dy]
    greeted += [at(k, 0) for k in range(1, nx)]
    greeted += [at(0, k) for k in range(1, ny)]
    for other in greeted:
        pl.semaphore_signal(barrier, inc=1, device_id=other, device_id_type=MESH)

    moves = [moves_s[0, 0, r] for r in range(ROWS)]
    rims = [rims_s[0, 0, m] for m in range(HALO)]
    row_for, slot_for = [], []
    for dx, dy in DIRS:
        ox, oy = at(dx, dy)
        brick = ox * ny + oy
        row, slot = jnp.int32(0), jnp.int32(-1)
        for r in range(ROWS):
            hit = (moves[r] >> 3) == brick
            row = jnp.where(hit, r, row)
            slot = jnp.where(hit, moves[r] & 7, slot)
        row_for.append(row)
        slot_for.append(slot)

    for m in range(HALO):
        info[pl.ds(m, 1), :] = meta[pl.ds(rims[m], 1), :]
        info[pl.ds(HALO + m, 1), :] = jnp.full((1, 128), rims[m], i32)
    for d in range(8):
        info[pl.ds(8 + d, 1), :] = jnp.full((1, 128), slot_for[d], i32)

    for role, n in ((I, 3 + (inner + 1) // 2), (Y, 3 + (cross + 1) // 2), (ZM, 1), (ZP, 6),
                    (ZMI, inner + 1), (ZPI, inner + 6), (ZMY, cross + 1), (ZPY, cross + 6)):
        role_s[role] = jnp.int32(ROWS) + HALO * n

    pl.semaphore_wait(barrier, len(greeted))

    sends = []
    for d, (dx, dy) in enumerate(DIRS):
        copy = pltpu.make_async_remote_copy(
            src_ref=info, dst_ref=infos.at[7 - d], send_sem=info_send.at[d], recv_sem=info_recv.at[7 - d],
            device_id=at(dx, dy), device_id_type=MESH)
        copy.start()
        sends.append(copy)
    load.wait()
    for d, (dx, dy) in enumerate(DIRS):
        stage[d] = dens[row_for[d]]
        copy = pltpu.make_async_remote_copy(
            src_ref=stage.at[d], dst_ref=mig.at[7 - d], send_sem=mig_send.at[d], recv_sem=mig_recv.at[7 - d],
            device_id=at(dx, dy), device_id_type=MESH)
        copy.start()
        sends.append(copy)

    flat = meta[8:16, :]
    sub = lax.broadcasted_iota(i32, (8, 128), 0)

    def matched(ids):
        found = jnp.full((8, 128), SLOTS, i32)
        for u in range(SLOTS):
            found = jnp.where(ids[:, u:u + 1] == flat, u, found)
        return found

    tab[0:8, :] = matched(meta[0:8, :])
    for group in range(POOL // 8):
        found = jnp.full((8, 128), SLOTS, i32)
        for t in range(SLOTS):
            found = jnp.where(meta[16 + t:17 + t, :] == sub + 8 * group, t, found)
        tab[POOL + 8 * group:POOL + 8 * group + 8, :] = found
    for d in range(8):
        sends[d].wait_recv()
    source = jnp.zeros((8, 128), i32)
    for n in range(8):
        dx, dy = DIRS[n]
        ids = infos[n, 0:8, :]
        pos = jnp.full((8, 128), -1, i32)
        for m in range(HALO):
            pos = jnp.where(ids == infos[n, HALO + m:HALO + m + 1, :], ROWS + HALO * n + m, pos)
        for n2, (ex, ey) in enumerate(DIRS):
            there = (dx + ex, dy + ey)
            first = ROWS + HALO * n2
            if there == (0, 0):
                for m in range(HALO):
                    pos = jnp.where(ids == first + m, rims[m], pos)
            elif there in DIRS:
                shift = HALO * (DIRS.index(there) - n2)
                pos = jnp.where((ids >= first) & (ids < first + HALO), ids + shift, pos)
        tab[ROWS + HALO * n:ROWS + HALO * n + HALO, :] = matched(pos)[:HALO]
        source = jnp.where(infos[n, 8 + 7 - n:9 + 7 - n, :] == sub, n, source)
    tab[2 * POOL:2 * POOL + 8, :] = source
    to_smem = pltpu.make_async_copy(tab, tab_s, tab_sem)
    to_smem.start()

    for g in range(ROWS):
        left[g * (SLOTS + 1) + SLOTS] = jnp.zeros((BLOCK, 256), bf16)
    for k in range(4):
        prod[k * (PAIRS + 1) + PAIRS] = jnp.zeros((ROWS, BLOCK, 128), f32)
    to_smem.wait()

    for d in range(8):
        sends[8 + d].wait_recv()

    def settle(r, carry):
        home, own = jnp.int32(0), jnp.int32(0)
        for q in range(ROWS):
            hit = moves[q] == me * ROWS + r
            home = jnp.where(hit, 1, home)
            own = jnp.where(hit, q, own)
        cur[0, r] = jnp.where(home == 1, dens[own], mig[tab_s[2 * POOL + r, 0]])
        return carry

    lax.fori_loop(0, ROWS, settle, 0)

    lane = lax.broadcasted_iota(i32, (8, 128), 1)
    low = (lax.broadcasted_iota(i32, (BLOCK, 128), 1) < BLOCK)
    eye = (lax.broadcasted_iota(i32, (BLOCK, 128), 1) == lax.broadcasted_iota(i32, (BLOCK, 128), 0))
    halves = lane // BLOCK

    def trace_of(chunk):
        return jnp.sum(jnp.where(eye, chunk, 0.0), axis=0, keepdims=True)

    def split_rows(step):
        def one(g, total):
            for q in range(PAIRS):
                chunk = cur[step, g, :, 128 * q:128 * q + 128]
                turned = pltpu.roll(chunk, BLOCK, 1)
                for odd in range(2):
                    twice = jnp.where(low, turned, chunk) if odd else jnp.where(low, chunk, turned)
                    hi = twice.astype(bf16)
                    lo = (twice - hi.astype(f32)).astype(bf16)
                    left[g * (SLOTS + 1) + 2 * q + odd, :, 0:128] = hi
                    left[g * (SLOTS + 1) + 2 * q + odd, :, 128:256] = lo
            return total + trace_of(cur[step, g, :, 0:128])

        return lax.fori_loop(0, ROWS, one, jnp.zeros((1, 128), f32))

    def multiply(strip, h, k):
        hi = strip.astype(bf16)
        lo = (strip - hi.astype(f32)).astype(bf16)
        right = jnp.concatenate([hi, lo, hi, lo], axis=0)
        rows = jnp.concatenate(
            [left[g * (SLOTS + 1) + tab_s[POOL + h, g]] for g in range(ROWS)], axis=0)
        for part in range(4):
            out = jnp.dot(rows, right[:, 256 * part:256 * part + 256], preferred_element_type=f32)
            prod[k * (PAIRS + 1) + 2 * part] = out[:, 0:128].reshape(ROWS, BLOCK, 128)
            prod[k * (PAIRS + 1) + 2 * part + 1] = out[:, 128:256].reshape(ROWS, BLOCK, 128)

    def gather(hs, first):
        def one(g, carry):
            for s in range(SLOTS):
                index = g * SLOTS + s
                total = None if first else acc[index].reshape(8, 8, 128)
                for k in range(4):
                    code = tab_s[hs[k], index]
                    block = prod[k * (PAIRS + 1) + (code >> 1), g].reshape(8, 8, 128)
                    block = jnp.where((halves == (code & 1))[None], block, 0.0)
                    total = block if total is None else total + block
                acc[index] = total.reshape(BLOCK, 128)
            return carry

        lax.fori_loop(0, ROWS, one, 0)

    def own_group(step, group, first):
        def one(k, carry):
            multiply(cur[step, 4 * group + k], 4 * group + k, k)
            return carry

        lax.fori_loop(0, 4, one, 0)
        gather([4 * group + k for k in range(4)], first)

    def halo_copy(step, src, role, m, target):
        place = role * HALO + m
        return pltpu.make_async_remote_copy(
            src_ref=src, dst_ref=near.at[step, place], send_sem=halo_send.at[step, place],
            recv_sem=halo_recv.at[step, place], device_id=target, device_id_type=MESH)

    def arrival(step, role, m):
        return halo_copy(step, near.at[step, role * HALO + m], role, m, at(0, 1))

    def pass_on(step, m):
        out = []
        for role, inside, outside in ((ZM, ZMI, ZMY), (ZP, ZPI, ZPY)):
            arrival(step, role, m).wait_recv()
            src = near.at[step, role * HALO + m]
            if m < HALO - 1:
                out.append(halo_copy(step, src, outside, m, at(0, cross)))
            out.append(halo_copy(step, src, inside, m, at(0, inner)))
        for copy in out:
            copy.start()
        return out

    def pass_on_last(step):
        m = HALO - 1
        arrival(step, Y, m).wait_recv()
        src = near.at[step, Y * HALO + m]
        out = [halo_copy(step, src, ZPY, m, at(-1, 0)), halo_copy(step, src, ZMY, m, at(1, 0))]
        for copy in out:
            copy.start()
        return out

    traces = []
    for step in range(2):
        for m in range(HALO):
            halo[step, m] = cur[step, rims[m]]
        out = []
        for m in (3, 0, 1, 2):
            src = halo.at[step, m]
            out.append(halo_copy(step, src, Y, m, at(0, cross)))
        for m in range(HALO):
            src = halo.at[step, m]
            out.append(halo_copy(step, src, ZP, m, at(-1, 0)))
            out.append(halo_copy(step, src, ZM, m, at(1, 0)))
        for m in range(HALO):
            out.append(halo_copy(step, halo.at[step, m], I, m, at(0, inner)))
        for copy in out:
            copy.start()
        before = split_rows(step)
        if step == 0:
            traces.append(before)
        own_group(step, 0, True)
        out += pass_on_last(step)
        out += pass_on(step, 0)
        own_group(step, 1, False)

        def near_group(q):
            places, hs = [], []
            for k in range(4):
                role = 2 * (q // 2) + k % 2
                m = 2 * (q % 2) + k // 2
                places.append(role * HALO + m)
                hs.append(role_s[role] + m)
            for k in range(4):
                role = 2 * (q // 2) + k % 2
                m = 2 * (q % 2) + k // 2
                if role in (ZM, ZP) or (role == Y and m == HALO - 1):
                    continue
                arrival(step, role, m).wait_recv()
            base = places[0]

            def one(k, carry):
                odd = lax.rem(k, 2)
                m = k // 2
                place = base + odd * HALO + m
                h = role_s[2 * (q // 2) + odd] + 2 * (q % 2) + m
                multiply(near[step, place], h, k)
                return carry

            lax.fori_loop(0, 4, one, 0)
            gather(hs, False)

        near_group(0)
        out += pass_on(step, 1)
        near_group(1)
        out += pass_on(step, 2)
        near_group(2)
        out += pass_on(step, 3)
        for q in range(3, 8):
            near_group(q)

        def finish(g, total):
            for q in range(PAIRS):
                even = acc[g * SLOTS + 2 * q]
                odd = acc[g * SLOTS + 2 * q + 1]
                squared = jnp.where(low, even + pltpu.roll(even, BLOCK, 1), odd + pltpu.roll(odd, BLOCK, 1))
                if q == 0:
                    total = total + trace_of(squared)
                if step == 0:
                    cur[1, g, :, 128 * q:128 * q + 128] = squared
                else:
                    outbuf[g, :, 128 * q:128 * q + 128] = 2.0 * cur[1, g, :, 128 * q:128 * q + 128] - squared
            return total

        traces.append(lax.fori_loop(0, ROWS, finish, jnp.zeros((1, 128), f32)))
        sends += out

    write = pltpu.make_async_copy(outbuf, out_hbm.at[0, 0], out_sem)
    write.start()

    row = jnp.concatenate([traces[0], traces[1], traces[1], traces[2], jnp.zeros((4, 128), f32)], axis=0)

    def exchange(value, buffer, index, count, send, recv, target):
        parts[...] = value
        buffer[index] = value
        copies = []
        for k in range(1, count):
            copies.append(pltpu.make_async_remote_copy(
                src_ref=parts, dst_ref=buffer.at[index], send_sem=send.at[k], recv_sem=recv.at[k],
                device_id=target(k), device_id_type=MESH))
        for copy in copies:
            copy.start()
        for copy in copies:
            copy.wait()
        total = buffer[0]
        for k in range(1, count):
            total = total + buffer[k]
        return total

    row = exchange(row, sum_y, iy, ny, sumy_send, sumy_recv, lambda k: at(0, k))
    row = exchange(row, sum_x, ix, nx, sumx_send, sumx_recv, lambda k: at(k, 0))
    scale = 1.0 / (nx * ny * ROWS * BLOCK)
    for k in range(4):
        occ_s[k] = jnp.sum(row[k:k + 1, :]) * scale

    for d in range(16):
        sends[d].wait_send()
    for copy in sends[16:]:
        copy.wait_send()
    write.wait()


def shards(nx, ny, density, moves, cols, halo_rows):
    mine = cols.reshape(ROWS, SLOTS)
    meta = jnp.concatenate([
        jnp.pad(mine, ((0, 0), (0, 128 - SLOTS)), constant_values=-1),
        jnp.broadcast_to(mine.reshape(1, ROWS * SLOTS), (8, 128)),
        jnp.pad(mine.T, ((0, 0), (0, 128 - ROWS)), constant_values=-1),
    ], axis=0)
    dma = pltpu.SemaphoreType.DMA
    vmem = pltpu.VMEM
    smem_spec = pl.BlockSpec(memory_space=pltpu.SMEM)
    return pl.pallas_call(
        functools.partial(kernel, nx, ny),
        out_shape=(jax.ShapeDtypeStruct(density.shape, f32), jax.ShapeDtypeStruct((4,), f32)),
        in_specs=[smem_spec, smem_spec, pl.BlockSpec(memory_space=vmem), pl.BlockSpec(memory_space=pl.ANY)],
        out_specs=(pl.BlockSpec(memory_space=pl.ANY), smem_spec),
        scratch_shapes=[
            vmem((ROWS, BLOCK, STRIP), f32),
            vmem((8, BLOCK, STRIP), f32),
            vmem((8, BLOCK, STRIP), f32),
            vmem((2, ROWS, BLOCK, STRIP), f32),
            vmem((2, HALO, BLOCK, STRIP), f32),
            vmem((2, 8 * HALO, BLOCK, STRIP), f32),
            vmem((ROWS * (SLOTS + 1), BLOCK, 256), bf16),
            vmem((4 * (PAIRS + 1), ROWS, BLOCK, 128), f32),
            vmem((ROWS * SLOTS, BLOCK, 128), f32),
            vmem((ROWS, BLOCK, STRIP), f32),
            vmem((16, 128), i32),
            vmem((8, 16, 128), i32),
            vmem((2 * POOL + 8, 128), i32),
            pltpu.SMEM((2 * POOL + 8, 128), i32),
            pltpu.SMEM((8,), i32),
            vmem((8, 128), f32),
            vmem((ny, 8, 128), f32),
            vmem((nx, 8, 128), f32),
            dma, dma, dma,
            dma((8,)), dma((8,)), dma((8,)), dma((8,)),
            dma((2, 8 * HALO)), dma((2, 8 * HALO)),
            dma((ny,)), dma((ny,)), dma((nx,)), dma((nx,)),
        ],
        compiler_params=pltpu.CompilerParams(
            collective_id=0, has_side_effects=True, vmem_limit_bytes=60 * 1024 * 1024),
    )(moves, halo_rows, meta, density)


def solution(mesh):
    nx, ny = mesh.shape["gx"], mesh.shape["gy"]
    in_specs = (
        P("gx", "gy", None, None, None),
        P("gx", "gy", None),
        P("gx", "gy", None, None),
        P("gx", "gy", None),
    )
    out_specs = (P("gx", "gy", None, None, None), P())
    return jax.shard_map(functools.partial(shards, nx, ny), mesh=mesh, in_specs=in_specs, out_specs=out_specs,
                         check_vma=False)
```

time: 1300 us -> 138 us (0.11); the launches traced: 1280 us -> 138 us
  local copies, waits for them, and re-layouts: 712 us -> 5.21 us
  waiting for transfers between devices: 224 us -> 0 us
  other arithmetic: 169 us -> 1.29 us
  Pallas kernels: 0 us -> 131 us
  matrix products: 74.5 us -> 0 us
  blocking collectives: 65.7 us -> 0 us
  starting transfers between devices: 37 us -> 0 us
    reshape x15 -> x1, local copies, waits for them, and re-layouts: 341 us -> 0.76 us  [shards(): mine = cols.reshape(ROWS, SLOTS)]
    gather x22 -> x0, local copies, waits for them, and re-layouts: 237 us -> none  [the longest x8 173 us: one_group(): jnp.take_along_axis(far_blocks, picked[:, :, None, :, None], axis=3)]
    ppermute x24 -> x0, waiting for transfers between devices: 224 us -> none  [the longest x12 196 us: extended_2(): lax.ppermute(lax.slice_in_dim(block, 0, width, axis=dim), axis, backward)]
    pallas_call x0 -> x1, Pallas kernels: none -> 131 us  [shards(): pl.pallas_call(functools.partial(kernel, nx, ny), out_shape=(jax.ShapeDty...]
    select_n x4 -> x0, local copies, waits for them, and re-layouts: 102 us -> none  [one_group(): jnp.where(found[:, :, None, :, None], aligned, 0.0)]
    select_n x16 -> x0, other arithmetic: 101 us -> none  [the longest x4 51.2 us: one_group(): jnp.where(found[:, :, None, :, None], aligned, 0.0)]
    dot_general x7 -> x0, matrix products: 74.5 us -> none  [the longest x4 64.8 us: one_group(): return jnp.einsum('gatb,gtbx->gax', mine, aligned, precision=highest)]
    psum x1 -> x0, blocking collectives: 65.7 us -> none  [shards(): results.append(lax.psum(pair, ('gx', 'gy')))]
  transfers between devices with their start and end apart: 24 -> 0, of which waited for: 16 -> 0; matrix products, arithmetic and copies ran while one was open for 1% -> 0% of each run, Pallas kernels for 0% -> 0%
where the time goes in v1:
time: 138 us
  Pallas kernels  131 us (95%)
  local copies, waits for them, and re-layouts  5.21 us (4%)
    pallas_call x1, Pallas kernels, shards(): pl.pallas_call(functools.partial(kernel, nx, ny), out_shape=(jax.ShapeDty...  131 us
    unnamed x4, local copies, waits for them, and re-layouts  3.68 us

profile of v1, /device:TPU:1, one launch (start us, length us, event | category | flops | bytes accessed | tf_op | source)
XLA Modules:
  0.0 137.8 jit_solution(11561202250634963149)
XLA Ops:
  0.6 0.8 broadcast_in_dim.7
  1.4 0.8 copy.6
  2.2 1.3 select_add_fusion.meta
  3.5 130.7 %shard_map.59 = (f32[1,1,8,64,1024]{4,3,2,1,0:T(8,128)}, f32[4]{0:T(128)}) custom-call(s32[1,1,8]{2,1,0:T(1,128)} %moves_s.1, s32[1,1,4]{2,1,0:T(1,128)} %rims_s.1, s32[32,128]{1,0:T(8,128)} %select_add_fusion.meta, f32[1,1,8,64,1024]{4,3,2,1,0:T(8,128)} %dens_hbm.1), custom_call_target="tpu_custom_call" | custom-call | tf_op jit(solution)/shard_map/pallas_call | solution.py:360
  134.1 0.0 copy-start
  134.2 3.2 %copy.9 = f32[1,1,8,64,1024]{4,3,2,1,0:T(8,128)} copy(f32[1,1,8,64,1024]{4,3,2,1,0:T(8,128)} %get-tuple-element.4) | data formatting | bytes 4194304
  137.3 0.0 copy-done
  137.3 0.5 copy.10
  (1 shorter events, 0.0 us)
Async XLA Ops:
  134.1 3.2 %copy-start = (f32[4]{0:T(128)S(1)}, f32[4]{0:T(128)}, u32[]{:S(2)}) copy-start(f32[4]{0:T(128)} %get-tuple-element.5) | copy-start | bytes 52

commit v2 on v1

v2 whole, which is shorter than its diff:
```python
import functools

import jax
import jax.numpy as jnp
from jax import lax
from jax.experimental import pallas as pl
from jax.experimental.pallas import tpu as pltpu
from jax.sharding import PartitionSpec as P

MESH = pl.DeviceIdType.MESH
f32 = jnp.float32
bf16 = jnp.bfloat16
i32 = jnp.int32

DIRS = ((-1, -1), (-1, 0), (-1, 1), (0, -1), (0, 1), (1, -1), (1, 0), (1, 1))

ROWS = 8
SLOTS = 16
BLOCK = 64
HALO = 4
STRIP = SLOTS * BLOCK
PAIRS = SLOTS // 2
POOL = ROWS + 8 * HALO

PLACE = tuple(4 * (s // 4) + (0, 2, 1, 3)[s % 4] for s in range(SLOTS))

I, Y, ZM, ZP, ZMI, ZPI, ZMY, ZPY = range(8)


def kernel(nx, ny, moves_s, rims_s, cols, dens_hbm, out_hbm, occ_s,
           dens, stage, mig, cur, halo, near, left, prod, acc,
           info, infos, tab, tab_s, role_s, parts, sum_y, sum_x,
           local_sem, tab_sem, out_sem, mig_send, mig_recv, info_send, info_recv,
           halo_send, halo_recv, sumy_send, sumy_recv, sumx_send, sumx_recv):
    ix = lax.axis_index("gx")
    iy = lax.axis_index("gy")
    me = ix * ny + iy
    cross = 2 * lax.rem(iy, 2) - 1
    inner = -cross

    def at(dx, dy):
        return (lax.rem(ix + dx + nx, nx), lax.rem(iy + dy + ny, ny))

    load = pltpu.make_async_copy(dens_hbm.at[0, 0], dens, local_sem)
    load.start()

    barrier = pltpu.get_barrier_semaphore()
    greeted = [at(dx, dy) for dx, dy in DIRS if dx and dy]
    greeted += [at(k, 0) for k in range(1, nx)]
    greeted += [at(0, k) for k in range(1, ny)]
    for other in greeted:
        pl.semaphore_signal(barrier, inc=1, device_id=other, device_id_type=MESH)

    moves = [moves_s[0, 0, r] for r in range(ROWS)]
    rims = [rims_s[0, 0, m] for m in range(HALO)]
    row_for, slot_for = [], []
    for dx, dy in DIRS:
        ox, oy = at(dx, dy)
        brick = ox * ny + oy
        row, slot = jnp.int32(0), jnp.int32(-1)
        for r in range(ROWS):
            hit = (moves[r] >> 3) == brick
            row = jnp.where(hit, r, row)
            slot = jnp.where(hit, moves[r] & 7, slot)
        row_for.append(row)
        slot_for.append(slot)

    info[...] = jnp.full((16, 128), -1, i32)
    for m in range(HALO):
        info[pl.ds(m, 1), 0:SLOTS] = cols[0, 0, pl.ds(rims[m], 1), :]
        info[pl.ds(HALO + m, 1), :] = jnp.full((1, 128), rims[m], i32)
    for d in range(8):
        info[pl.ds(8 + d, 1), :] = jnp.full((1, 128), slot_for[d], i32)

    for role, n in ((I, 3 + (inner + 1) // 2), (Y, 3 + (cross + 1) // 2), (ZM, 1), (ZP, 6),
                    (ZMI, inner + 1), (ZPI, inner + 6), (ZMY, cross + 1), (ZPY, cross + 6)):
        role_s[role] = jnp.int32(ROWS) + HALO * n

    pl.semaphore_wait(barrier, len(greeted))

    def turn_row(src, dst):
        for q in range(4):
            tile = jnp.concatenate([src[:, 256 * q:256 * q + 128], src[:, 256 * q + 128:256 * q + 256]], axis=0)
            turned = jnp.transpose(tile)
            dst[:, 256 * q:256 * q + 128] = turned[0:BLOCK]
            dst[:, 256 * q + 128:256 * q + 256] = turned[BLOCK:]

    sends = []
    for d, (dx, dy) in enumerate(DIRS):
        copy = pltpu.make_async_remote_copy(
            src_ref=info, dst_ref=infos.at[7 - d], send_sem=info_send.at[d], recv_sem=info_recv.at[7 - d],
            device_id=at(dx, dy), device_id_type=MESH)
        copy.start()
        sends.append(copy)
    load.wait()
    for d, (dx, dy) in enumerate(DIRS):
        turn_row(dens.at[row_for[d]], stage.at[d])
        copy = pltpu.make_async_remote_copy(
            src_ref=stage.at[d], dst_ref=mig.at[7 - d], send_sem=mig_send.at[d], recv_sem=mig_recv.at[7 - d],
            device_id=at(dx, dy), device_id_type=MESH)
        copy.start()
        sends.append(copy)

    def turn(r, carry):
        turn_row(dens.at[r], dens.at[r])
        return carry

    lax.fori_loop(0, ROWS, turn, 0)

    flat = jnp.broadcast_to(
        jnp.concatenate([cols[0, 0, g:g + 1, :] for g in range(ROWS)], axis=1), (8, 128))
    slot = lax.rem(lax.broadcasted_iota(i32, (8, 128), 1), SLOTS)
    middle = lax.rem(slot, 4)
    place = slot + jnp.where(middle == 1, 1, 0) - jnp.where(middle == 2, 1, 0)
    sub = lax.broadcasted_iota(i32, (8, 128), 0)

    def matched(ids):
        found = jnp.full((8, 128), SLOTS, i32)
        for u in range(SLOTS):
            found = jnp.where(ids[:, u:u + 1] == flat, PLACE[u], found)
        return found

    tab[0:8, :] = matched(cols[0, 0])
    for group in range(POOL // 8):
        found = jnp.where(flat == sub + 8 * group, place - SLOTS, 0)
        for width in (1, 2, 4, 8):
            found = found + pltpu.roll(found, 128 - width, 1)
        found = jnp.clip(found + SLOTS, 0, SLOTS)
        tab[POOL + 8 * group:POOL + 8 * group + 8, :] = found
    for d in range(8):
        sends[d].wait_recv()
    source = jnp.zeros((8, 128), i32)
    for n in range(8):
        dx, dy = DIRS[n]
        ids = infos[n, 0:8, :]
        pos = jnp.full((8, 128), -1, i32)
        for m in range(HALO):
            pos = jnp.where(ids == infos[n, HALO + m:HALO + m + 1, :], ROWS + HALO * n + m, pos)
        for n2, (ex, ey) in enumerate(DIRS):
            there = (dx + ex, dy + ey)
            first = ROWS + HALO * n2
            if there == (0, 0):
                for m in range(HALO):
                    pos = jnp.where(ids == first + m, rims[m], pos)
            elif there in DIRS:
                shift = HALO * (DIRS.index(there) - n2)
                pos = jnp.where((ids >= first) & (ids < first + HALO), ids + shift, pos)
        tab[ROWS + HALO * n:ROWS + HALO * n + HALO, :] = matched(pos)[:HALO]
        source = jnp.where(infos[n, 8 + 7 - n:9 + 7 - n, :] == sub, n, source)
    tab[2 * POOL:2 * POOL + 8, :] = source
    to_smem = pltpu.make_async_copy(tab, tab_s, tab_sem)
    to_smem.start()

    for g in range(ROWS):
        left[g * (SLOTS + 1) + SLOTS] = jnp.zeros((128, 128), bf16)
    for k in range(4):
        prod[k * (SLOTS + 1) + SLOTS] = jnp.zeros((ROWS // 2, BLOCK, 128), f32)
    to_smem.wait()

    for d in range(8):
        sends[8 + d].wait_recv()

    def settle(r, carry):
        home, own = jnp.int32(0), jnp.int32(0)
        for q in range(ROWS):
            hit = moves[q] == me * ROWS + r
            home = jnp.where(hit, 1, home)
            own = jnp.where(hit, q, own)
        cur[0, r] = jnp.where(home == 1, dens[own], mig[tab_s[2 * POOL + r, 0]])
        return carry

    lax.fori_loop(0, ROWS, settle, 0)

    lanes = lax.broadcasted_iota(i32, (BLOCK, 128), 1)
    low = lanes < BLOCK
    low_wide = lax.broadcasted_iota(i32, (128, 128), 1) < BLOCK
    eye = lax.broadcasted_iota(i32, (BLOCK, 128), 0)
    eye_low = lanes == eye
    eye_both = lax.rem(lanes, BLOCK) == eye

    def trace_of(chunk, where):
        return jnp.sum(jnp.where(where, chunk, 0.0), axis=0, keepdims=True)

    def split_rows(step):
        def one(g, total):
            for q in range(PAIRS):
                chunk = cur[step, g, :, 128 * q:128 * q + 128]
                turned = pltpu.roll(chunk, BLOCK, 1)
                for odd in range(2):
                    twice = jnp.where(low, turned, chunk) if odd else jnp.where(low, chunk, turned)
                    hi = twice.astype(bf16)
                    lo = (twice - hi.astype(f32)).astype(bf16)
                    left[g * (SLOTS + 1) + 2 * q + odd, 0:BLOCK, :] = hi
                    left[g * (SLOTS + 1) + 2 * q + odd, BLOCK:128, :] = lo
            return total + trace_of(cur[step, g, :, 0:128], eye_low)

        return lax.fori_loop(0, ROWS, one, jnp.zeros((1, 128), f32))

    def multiply(strip, h, k):
        blocks = []
        for pair in range(ROWS // 2):
            even = left[2 * pair * (SLOTS + 1) + tab_s[POOL + h, SLOTS * 2 * pair]]
            odd = left[(2 * pair + 1) * (SLOTS + 1) + tab_s[POOL + h, SLOTS * (2 * pair + 1)]]
            blocks.append(jnp.where(low_wide, even, odd))
        weights = jnp.concatenate(blocks, axis=1)
        weights = jnp.concatenate([weights[0:BLOCK], weights[0:BLOCK], weights[BLOCK:], weights[BLOCK:]], axis=0)
        far = []
        for q in range(PAIRS):
            chunk = strip[:, 128 * q:128 * q + 128]
            hi = chunk.astype(bf16).astype(f32)
            lo = chunk - hi
            far.append(jnp.where(low, hi, pltpu.roll(lo, BLOCK, 1)).astype(bf16))
            far.append(jnp.where(low, pltpu.roll(hi, BLOCK, 1), lo).astype(bf16))
        far = jnp.concatenate(far, axis=0)
        far = jnp.concatenate([far, far], axis=1)
        for part in range(2):
            out = jnp.dot(far, weights[:, 256 * part:256 * part + 256], preferred_element_type=f32)
            for u in range(SLOTS):
                for half in range(2):
                    prod[k * (SLOTS + 1) + u, 2 * part + half] = out[
                        BLOCK * u:BLOCK * u + BLOCK, 128 * half:128 * half + 128]

    def gather(hs, fresh):
        def one(pair, carry):
            for s in range(SLOTS):
                index = pair * SLOTS + s
                total = acc[index]
                if fresh is not None:
                    total = jnp.where(fresh, 0.0, total)
                for k in range(4):
                    even = prod[k * (SLOTS + 1) + tab_s[hs[k], 2 * SLOTS * pair + s], pair]
                    odd = prod[k * (SLOTS + 1) + tab_s[hs[k], 2 * SLOTS * pair + SLOTS + s], pair]
                    total = total + jnp.where(low, even, odd)
                acc[index] = total
            return carry

        lax.fori_loop(0, ROWS // 2, one, 0)

    def group(strips, hs, fresh=None):
        for k in range(4):
            multiply(strips[k], hs[k], k)
        gather(hs, fresh)

    def halo_copy(step, src, role, m, target):
        place = role * HALO + m
        return pltpu.make_async_remote_copy(
            src_ref=src, dst_ref=near.at[step, place], send_sem=halo_send.at[step, place],
            recv_sem=halo_recv.at[step, place], device_id=target, device_id_type=MESH)

    def arrival(step, role, m):
        return halo_copy(step, near.at[step, role * HALO + m], role, m, at(0, 1))

    def passed_on(step, m):
        out = []
        for role, inside, outside in ((ZM, ZMI, ZMY), (ZP, ZPI, ZPY)):
            src = near.at[step, role * HALO + m]
            if m < HALO - 1:
                out.append(halo_copy(step, src, outside, m, at(0, cross)))
            out.append(halo_copy(step, src, inside, m, at(0, inner)))
        return out

    def passed_on_last(step):
        src = near.at[step, Y * HALO + HALO - 1]
        return [halo_copy(step, src, ZPY, HALO - 1, at(-1, 0)), halo_copy(step, src, ZMY, HALO - 1, at(1, 0))]

    def pass_on(step, m):
        arrival(step, ZM, m).wait_recv()
        arrival(step, ZP, m).wait_recv()
        for copy in passed_on(step, m):
            copy.start()

    def pass_on_last(step):
        arrival(step, Y, HALO - 1).wait_recv()
        for copy in passed_on_last(step):
            copy.start()

    traces = []
    for step in range(2):
        for m in range(HALO):
            halo[step, m] = cur[step, rims[m]]
        out = []
        for m in (3, 0, 1, 2):
            src = halo.at[step, m]
            out.append(halo_copy(step, src, Y, m, at(0, cross)))
        for m in range(HALO):
            src = halo.at[step, m]
            out.append(halo_copy(step, src, ZP, m, at(-1, 0)))
            out.append(halo_copy(step, src, ZM, m, at(1, 0)))
        for m in range(HALO):
            out.append(halo_copy(step, halo.at[step, m], I, m, at(0, inner)))
        for copy in out:
            copy.start()
        before = split_rows(step)
        if step == 0:
            traces.append(before)

        def own_group(i, carry):
            @pl.when(i == 1)
            def _():
                pass_on_last(step)
                pass_on(step, 0)

            group([cur.at[step, 4 * i + k] for k in range(4)], [4 * i + k for k in range(4)], i == 0)
            return carry

        lax.fori_loop(0, 2, own_group, 0)

        def near_group(q, carry):
            for m in range(1, HALO):
                @pl.when(q == m)
                def _():
                    pass_on(step, m)

            roles = [2 * (q // 2) + k % 2 for k in range(4)]
            ms = [2 * (q % 2) + k // 2 for k in range(4)]
            for k in range(4):
                waits = q // 2 != ZM // 2
                if k == 3:
                    waits = waits & (q != 1)

                @pl.when(waits)
                def _():
                    arrival(step, roles[k], ms[k]).wait_recv()

            group([near.at[step, roles[k] * HALO + ms[k]] for k in range(4)],
                  [role_s[roles[k]] + ms[k] for k in range(4)])
            return carry

        lax.fori_loop(0, 8, near_group, 0)

        total = jnp.zeros((1, 128), f32)
        for pair in range(ROWS // 2):
            total = total + trace_of(acc[pair * SLOTS], eye_both)
        traces.append(total)
        for m in range(HALO):
            out += passed_on(step, m)
        out += passed_on_last(step)
        sends += out

        def combine(pair, odd_row, q):
            first = acc[pair * SLOTS + PLACE[2 * q]]
            second = acc[pair * SLOTS + PLACE[2 * q + 1]]
            if odd_row:
                return jnp.where(low, pltpu.roll(first, BLOCK, 1), second)
            return jnp.where(low, first, pltpu.roll(second, BLOCK, 1))

        if step == 0:
            def finish(pair, carry):
                for odd_row in range(2):
                    for q in range(PAIRS):
                        cur[1, 2 * pair + odd_row, :, 128 * q:128 * q + 128] = combine(pair, odd_row, q)
                return carry

            lax.fori_loop(0, ROWS // 2, finish, 0)

    row = jnp.concatenate([traces[0], traces[1], traces[1], traces[2], jnp.zeros((4, 128), f32)], axis=0)

    def exchange(value, buffer, index, count, send, recv, target):
        parts[count % 3] = value
        buffer[index] = value
        copies = []
        for k in range(1, count):
            copies.append(pltpu.make_async_remote_copy(
                src_ref=parts.at[count % 3], dst_ref=buffer.at[index], send_sem=send.at[k], recv_sem=recv.at[k],
                device_id=target(k), device_id_type=MESH))
        for copy in copies:
            copy.start()
        return copies

    def exchanged(copies, buffer, count):
        for copy in copies:
            copy.wait_recv()
        total = buffer[0]
        for k in range(1, count):
            total = total + buffer[k]
        return total

    along_y = exchange(row, sum_y, iy, ny, sumy_send, sumy_recv, lambda k: at(0, k))

    def last(pair, carry):
        for odd_row in range(2):
            g = 2 * pair + odd_row
            for q in range(4):
                tiles = []
                for half in range(2):
                    chunk = cur[1, g, :, 256 * q + 128 * half:256 * q + 128 * half + 128]
                    tiles.append(2.0 * chunk - combine(pair, odd_row, 2 * q + half))
                turned = jnp.transpose(jnp.concatenate(tiles, axis=0))
                dens[g, :, 256 * q:256 * q + 128] = turned[0:BLOCK]
                dens[g, :, 256 * q + 128:256 * q + 256] = turned[BLOCK:]
        return carry

    lax.fori_loop(0, ROWS // 2, last, 0)
    write = pltpu.make_async_copy(dens, out_hbm.at[0, 0], out_sem)
    write.start()

    row = exchanged(along_y, sum_y, ny)
    along_x = exchange(row, sum_x, ix, nx, sumx_send, sumx_recv, lambda k: at(k, 0))
    row = exchanged(along_x, sum_x, nx)
    scale = 1.0 / (nx * ny * ROWS * BLOCK)
    for k in range(4):
        occ_s[k] = jnp.sum(row[k:k + 1, :]) * scale

    for d in range(16):
        sends[d].wait_send()
    for copy in sends[16:] + along_y + along_x:
        copy.wait_send()
    write.wait()


def shards(nx, ny, density, moves, cols, halo_rows):
    dma = pltpu.SemaphoreType.DMA
    vmem = pltpu.VMEM
    smem_spec = pl.BlockSpec(memory_space=pltpu.SMEM)
    return pl.pallas_call(
        functools.partial(kernel, nx, ny),
        out_shape=(jax.ShapeDtypeStruct(density.shape, f32), jax.ShapeDtypeStruct((4,), f32)),
        in_specs=[smem_spec, smem_spec, pl.BlockSpec(memory_space=vmem), pl.BlockSpec(memory_space=pl.ANY)],
        out_specs=(pl.BlockSpec(memory_space=pl.ANY), smem_spec),
        scratch_shapes=[
            vmem((ROWS, BLOCK, STRIP), f32),
            vmem((8, BLOCK, STRIP), f32),
            vmem((8, BLOCK, STRIP), f32),
            vmem((2, ROWS, BLOCK, STRIP), f32),
            vmem((2, HALO, BLOCK, STRIP), f32),
            vmem((2, 8 * HALO, BLOCK, STRIP), f32),
            vmem((ROWS * (SLOTS + 1), 128, 128), bf16),
            vmem((4 * (SLOTS + 1), ROWS // 2, BLOCK, 128), f32),
            vmem((ROWS // 2 * SLOTS, BLOCK, 128), f32),
            vmem((16, 128), i32),
            vmem((8, 16, 128), i32),
            vmem((2 * POOL + 8, 128), i32),
            pltpu.SMEM((2 * POOL + 8, 128), i32),
            pltpu.SMEM((8,), i32),
            vmem((3, 8, 128), f32),
            vmem((ny, 8, 128), f32),
            vmem((nx, 8, 128), f32),
            dma, dma, dma,
            dma((8,)), dma((8,)), dma((8,)), dma((8,)),
            dma((2, 8 * HALO)), dma((2, 8 * HALO)),
            dma((ny,)), dma((ny,)), dma((nx,)), dma((nx,)),
        ],
        compiler_params=pltpu.CompilerParams(
            collective_id=0, has_side_effects=True, vmem_limit_bytes=60 * 1024 * 1024),
    )(moves, halo_rows, cols, density)


def solution(mesh):
    nx, ny = mesh.shape["gx"], mesh.shape["gy"]
    in_specs = (
        P("gx", "gy", None, None, None),
        P("gx", "gy", None),
        P("gx", "gy", None, None),
        P("gx", "gy", None),
    )
    out_specs = (P("gx", "gy", None, None, None), P())
    return jax.shard_map(functools.partial(shards, nx, ny), mesh=mesh, in_specs=in_specs, out_specs=out_specs,
                         check_vma=False)
```

time: 138 us -> 126 us (0.913)
  Pallas kernels: 131 us -> 122 us
  local copies, waits for them, and re-layouts: 5.21 us -> 3.68 us
    pallas_call x1, Pallas kernels: 131 us -> 122 us  [shards(): pl.pallas_call(functools.partial(kernel, nx, ny), out_shape=(jax.ShapeDty...]
where the time goes in v2:
time: 126 us
  Pallas kernels  122 us (97%)
  local copies, waits for them, and re-layouts  3.68 us (3%)
    pallas_call x1, Pallas kernels, shards(): pl.pallas_call(functools.partial(kernel, nx, ny), out_shape=(jax.ShapeDty...  122 us
    unnamed x4, local copies, waits for them, and re-layouts  3.68 us

profile of v2, /device:TPU:1, one launch (start us, length us, event | category | flops | bytes accessed | tf_op | source)
XLA Modules:
  0.0 126.0 jit_solution(13747374472265005261)
XLA Ops:
  0.6 121.6 %shard_map.59 = (f32[1,1,8,64,1024]{4,3,2,1,0:T(8,128)}, f32[4]{0:T(128)}) custom-call(s32[1,1,8]{2,1,0:T(1,128)} %moves_s.1, s32[1,1,4]{2,1,0:T(1,128)} %rims_s.1, s32[1,1,8,16]{3,2,1,0:T(8,128)} %cols.1, f32[1,1,8,64,1024]{4,3,2,1,0:T(8,128)} %dens_hbm.1), custom_call_target="tpu_custom_call" | custom-call | tf_op jit(solution)/shard_map/pallas_call | solution.py:415
  122.3 0.0 copy-start
  122.3 3.2 %copy.8 = f32[1,1,8,64,1024]{4,3,2,1,0:T(8,128)} copy(f32[1,1,8,64,1024]{4,3,2,1,0:T(8,128)} %get-tuple-element.4) | data formatting | bytes 4194304
  125.5 0.0 copy-done
  125.5 0.5 copy.9
Async XLA Ops:
  122.3 3.2 %copy-start = (f32[4]{0:T(128)S(1)}, f32[4]{0:T(128)}, u32[]{:S(2)}) copy-start(f32[4]{0:T(128)} %get-tuple-element.5) | copy-start | bytes 52

commit v3 on v2

--- a/solution.py
+++ b/solution.py
@@ -25,6 +25,18 @@
 PLACE = tuple(4 * (s // 4) + (0, 2, 1, 3)[s % 4] for s in range(SLOTS))
 
 I, Y, ZM, ZP, ZMI, ZPI, ZMY, ZPY = range(8)
+
+ARRIVING = (
+    ((I, 0), (I, 1), (I, 2), (I, 3)),
+    ((Y, 3), (Y, 0), (ZM, 0), (ZP, 0)),
+    ((ZMI, 0), (ZPI, 0), (Y, 1), (Y, 2)),
+    ((ZM, 1), (ZP, 1), (ZMI, 1), (ZPI, 1)),
+    ((ZM, 2), (ZP, 2), (ZMY, 0), (ZPY, 0)),
+    ((ZMI, 2), (ZPI, 2), (ZM, 3), (ZP, 3)),
+    ((ZMI, 3), (ZPI, 3), (ZMY, 1), (ZPY, 1)),
+    ((ZMY, 2), (ZPY, 2), (ZMY, 3), (ZPY, 3)),
+)
+PASS_BEFORE = (0, 2, 4, 5)
 
 
 def kernel(nx, ny, moves_s, rims_s, cols, dens_hbm, out_hbm, occ_s,
@@ -160,16 +172,13 @@
     for d in range(8):
         sends[8 + d].wait_recv()
 
-    def settle(r, carry):
+    def arrived(r):
         home, own = jnp.int32(0), jnp.int32(0)
         for q in range(ROWS):
             hit = moves[q] == me * ROWS + r
             home = jnp.where(hit, 1, home)
             own = jnp.where(hit, q, own)
-        cur[0, r] = jnp.where(home == 1, dens[own], mig[tab_s[2 * POOL + r, 0]])
-        return carry
-
-    lax.fori_loop(0, ROWS, settle, 0)
+        return jnp.where(home == 1, dens[own], mig[tab_s[2 * POOL + r, 0]])
 
     lanes = lax.broadcasted_iota(i32, (BLOCK, 128), 1)
     low = lanes < BLOCK
@@ -220,9 +229,9 @@
                     prod[k * (SLOTS + 1) + u, 2 * part + half] = out[
                         BLOCK * u:BLOCK * u + BLOCK, 128 * half:128 * half + 128]
 
-    def gather(hs, fresh):
+    def gather(hs, fresh, slots=range(SLOTS)):
         def one(pair, carry):
-            for s in range(SLOTS):
+            for s in slots:
                 index = pair * SLOTS + s
                 total = acc[index]
                 if fresh is not None:
@@ -274,59 +283,93 @@
         for copy in passed_on_last(step):
             copy.start()
 
+    def chunk_of(pair, odd, q):
+        first = acc[pair * SLOTS + PLACE[2 * q]]
+        second = acc[pair * SLOTS + PLACE[2 * q + 1]]
+        if odd:
+            return jnp.where(low, pltpu.roll(first, BLOCK, 1), second)
+        return jnp.where(low, first, pltpu.roll(second, BLOCK, 1))
+
+    def combine(row, q):
+        return jnp.where((row & 1) == 1, chunk_of(row >> 1, True, q), chunk_of(row >> 1, False, q))
+
     traces = []
     for step in range(2):
+        out = []
+
+        def send(role, m, target):
+            out.append(halo_copy(step, halo.at[step, m], role, m, target))
+            out[-1].start()
+
+        for m in (3, 0, 1, 2):
+            if step == 0:
+                halo[step, m] = arrived(rims[m])
+            else:
+                for q in range(PAIRS):
+                    halo[step, m, :, 128 * q:128 * q + 128] = combine(rims[m], q)
+            send(Y, m, at(0, cross))
+            if m < 3:
+                send(ZP, m, at(-1, 0))
+                send(ZM, m, at(1, 0))
+        send(ZP, 3, at(-1, 0))
+        send(ZM, 3, at(1, 0))
         for m in range(HALO):
-            halo[step, m] = cur[step, rims[m]]
-        out = []
-        for m in (3, 0, 1, 2):
-            src = halo.at[step, m]
-            out.append(halo_copy(step, src, Y, m, at(0, cross)))
-        for m in range(HALO):
-            src = halo.at[step, m]
-            out.append(halo_copy(step, src, ZP, m, at(-1, 0)))
-            out.append(halo_copy(step, src, ZM, m, at(1, 0)))
-        for m in range(HALO):
-            out.append(halo_copy(step, halo.at[step, m], I, m, at(0, inner)))
-        for copy in out:
-            copy.start()
+            send(I, m, at(0, inner))
+
+        def settle(r, carry):
+            if step == 0:
+                cur[0, r] = arrived(r)
+            else:
+                for odd in range(2):
+                    for q in range(PAIRS):
+                        cur[1, 2 * r + odd, :, 128 * q:128 * q + 128] = chunk_of(r, odd, q)
+            return carry
+
+        lax.fori_loop(0, ROWS if step == 0 else ROWS // 2, settle, 0)
         before = split_rows(step)
         if step == 0:
             traces.append(before)
 
         def own_group(i, carry):
-            @pl.when(i == 1)
-            def _():
-                pass_on_last(step)
-                pass_on(step, 0)
-
             group([cur.at[step, 4 * i + k] for k in range(4)], [4 * i + k for k in range(4)], i == 0)
             return carry
 
         lax.fori_loop(0, 2, own_group, 0)
 
-        def near_group(q, carry):
-            for m in range(1, HALO):
-                @pl.when(q == m)
+        def near_strips(q):
+            for m in range(HALO):
+                @pl.when(q == PASS_BEFORE[m])
                 def _():
                     pass_on(step, m)
-
-            roles = [2 * (q // 2) + k % 2 for k in range(4)]
-            ms = [2 * (q % 2) + k // 2 for k in range(4)]
+                    if m == 0:
+                        pass_on_last(step)
+
+            strips, hs = [], []
             for k in range(4):
-                waits = q // 2 != ZM // 2
-                if k == 3:
-                    waits = waits & (q != 1)
-
-                @pl.when(waits)
+                roles = sum(four[k][0] << (3 * j) for j, four in enumerate(ARRIVING))
+                rows = sum(four[k][1] << (2 * j) for j, four in enumerate(ARRIVING))
+                waits = sum(int(not (four[k][0] in (ZM, ZP) or four[k] == (Y, 3))) << j for j, four in enumerate(ARRIVING))
+                role = (jnp.int32(roles) >> (3 * q)) & 7
+                m = (jnp.int32(rows) >> (2 * q)) & 3
+
+                @pl.when(((jnp.int32(waits) >> q) & 1) == 1)
                 def _():
-                    arrival(step, roles[k], ms[k]).wait_recv()
-
-            group([near.at[step, roles[k] * HALO + ms[k]] for k in range(4)],
-                  [role_s[roles[k]] + ms[k] for k in range(4)])
+                    arrival(step, role, m).wait_recv()
+
+                strips.append(near.at[step, role * HALO + m])
+                hs.append(role_s[role] + m)
+            return strips, hs
+
+        def near_group(q, carry):
+            group(*near_strips(q))
             return carry
 
-        lax.fori_loop(0, 8, near_group, 0)
+        lax.fori_loop(0, 8 if step == 0 else 7, near_group, 0)
+        if step == 1:
+            strips, hs = near_strips(jnp.int32(7))
+            for k in range(4):
+                multiply(strips[k], hs[k], k)
+            gather(hs, None, range(1))
 
         total = jnp.zeros((1, 128), f32)
         for pair in range(ROWS // 2):
@@ -336,22 +379,6 @@
             out += passed_on(step, m)
         out += passed_on_last(step)
         sends += out
-
-        def combine(pair, odd_row, q):
-            first = acc[pair * SLOTS + PLACE[2 * q]]
-            second = acc[pair * SLOTS + PLACE[2 * q + 1]]
-            if odd_row:
-                return jnp.where(low, pltpu.roll(first, BLOCK, 1), second)
-            return jnp.where(low, first, pltpu.roll(second, BLOCK, 1))
-
-        if step == 0:
-            def finish(pair, carry):
-                for odd_row in range(2):
-                    for q in range(PAIRS):
-                        cur[1, 2 * pair + odd_row, :, 128 * q:128 * q + 128] = combine(pair, odd_row, q)
-                return carry
-
-            lax.fori_loop(0, ROWS // 2, finish, 0)
 
     row = jnp.concatenate([traces[0], traces[1], traces[1], traces[2], jnp.zeros((4, 128), f32)], axis=0)
 
@@ -377,6 +404,8 @@
 
     along_y = exchange(row, sum_y, iy, ny, sumy_send, sumy_recv, lambda k: at(0, k))
 
+    gather(hs, None, range(1, SLOTS))
+
     def last(pair, carry):
         for odd_row in range(2):
             g = 2 * pair + odd_row
@@ -384,7 +413,7 @@
                 tiles = []
                 for half in range(2):
                     chunk = cur[1, g, :, 256 * q + 128 * half:256 * q + 128 * half + 128]
-                    tiles.append(2.0 * chunk - combine(pair, odd_row, 2 * q + half))
+                    tiles.append(2.0 * chunk - chunk_of(pair, odd_row, 2 * q + half))
                 turned = jnp.transpose(jnp.concatenate(tiles, axis=0))
                 dens[g, :, 256 * q:256 * q + 128] = turned[0:BLOCK]
                 dens[g, :, 256 * q + 128:256 * q + 256] = turned[BLOCK:]

time: 126 us -> 114 us (0.905)
  Pallas kernels: 122 us -> 110 us
    pallas_call x1, Pallas kernels: 122 us -> 110 us  [shards(): pl.pallas_call(functools.partial(kernel, nx, ny), out_shape=(jax.ShapeDty...]
where the time goes in v3:
time: 114 us
  Pallas kernels  110 us (96%)
  local copies, waits for them, and re-layouts  3.68 us (3%)
    pallas_call x1, Pallas kernels, shards(): pl.pallas_call(functools.partial(kernel, nx, ny), out_shape=(jax.ShapeDty...  110 us
    unnamed x4, local copies, waits for them, and re-layouts  3.68 us

profile of v3, /device:TPU:1, one launch (start us, length us, event | category | flops | bytes accessed | tf_op | source)
XLA Modules:
  0.0 113.9 jit_solution(2278232071681458326)
XLA Ops:
  0.6 109.6 %shard_map.59 = (f32[1,1,8,64,1024]{4,3,2,1,0:T(8,128)}, f32[4]{0:T(128)}) custom-call(s32[1,1,8]{2,1,0:T(1,128)} %moves_s.1, s32[1,1,4]{2,1,0:T(1,128)} %rims_s.1, s32[1,1,8,16]{3,2,1,0:T(8,128)} %cols.1, f32[1,1,8,64,1024]{4,3,2,1,0:T(8,128)} %dens_hbm.1), custom_call_target="tpu_custom_call" | custom-call | tf_op jit(solution)/shard_map/pallas_call | solution.py:444
  110.3 0.0 copy-start
  110.3 3.2 %copy.8 = f32[1,1,8,64,1024]{4,3,2,1,0:T(8,128)} copy(f32[1,1,8,64,1024]{4,3,2,1,0:T(8,128)} %get-tuple-element.4) | data formatting | bytes 4194304
  113.4 0.0 copy-done
  113.4 0.5 copy.9
Async XLA Ops:
  110.3 3.2 %copy-start = (f32[4]{0:T(128)S(1)}, f32[4]{0:T(128)}, u32[]{:S(2)}) copy-start(f32[4]{0:T(128)} %get-tuple-element.5) | copy-start | bytes 52

commit v4 on v3

--- a/solution.py
+++ b/solution.py
@@ -39,10 +39,10 @@
 PASS_BEFORE = (0, 2, 4, 5)
 
 
-def kernel(nx, ny, moves_s, rims_s, cols, dens_hbm, out_hbm, occ_s,
+def kernel(nx, ny, cols, dens_hbm, result, occ_s, cols_s,
            dens, stage, mig, cur, halo, near, left, prod, acc,
            info, infos, tab, tab_s, role_s, parts, sum_y, sum_x,
-           local_sem, tab_sem, out_sem, mig_send, mig_recv, info_send, info_recv,
+           local_sem, small_sem, tab_sem, mig_send, mig_recv, info_send, info_recv,
            halo_send, halo_recv, sumy_send, sumy_recv, sumx_send, sumx_recv):
     ix = lax.axis_index("gx")
     iy = lax.axis_index("gy")
@@ -55,6 +55,8 @@
 
     load = pltpu.make_async_copy(dens_hbm.at[0, 0], dens, local_sem)
     load.start()
+    small = pltpu.make_async_copy(cols, cols_s, small_sem)
+    small.start()
 
     barrier = pltpu.get_barrier_semaphore()
     greeted = [at(dx, dy) for dx, dy in DIRS if dx and dy]
@@ -63,8 +65,10 @@
     for other in greeted:
         pl.semaphore_signal(barrier, inc=1, device_id=other, device_id_type=MESH)
 
-    moves = [moves_s[0, 0, r] for r in range(ROWS)]
-    rims = [rims_s[0, 0, m] for m in range(HALO)]
+    small.wait()
+
+    moves = [cols_s[ROWS, r] for r in range(ROWS)]
+    rims = [cols_s[ROWS + 1, m] for m in range(HALO)]
     row_for, slot_for = [], []
     for dx, dy in DIRS:
         ox, oy = at(dx, dy)
@@ -79,7 +83,7 @@
 
     info[...] = jnp.full((16, 128), -1, i32)
     for m in range(HALO):
-        info[pl.ds(m, 1), 0:SLOTS] = cols[0, 0, pl.ds(rims[m], 1), :]
+        info[pl.ds(m, 1), 0:SLOTS] = cols[pl.ds(rims[m], 1), :]
         info[pl.ds(HALO + m, 1), :] = jnp.full((1, 128), rims[m], i32)
     for d in range(8):
         info[pl.ds(8 + d, 1), :] = jnp.full((1, 128), slot_for[d], i32)
@@ -87,8 +91,6 @@
     for role, n in ((I, 3 + (inner + 1) // 2), (Y, 3 + (cross + 1) // 2), (ZM, 1), (ZP, 6),
                     (ZMI, inner + 1), (ZPI, inner + 6), (ZMY, cross + 1), (ZPY, cross + 6)):
         role_s[role] = jnp.int32(ROWS) + HALO * n
-
-    pl.semaphore_wait(barrier, len(greeted))
 
     def turn_row(src, dst):
         for q in range(4):
@@ -96,6 +98,12 @@
             turned = jnp.transpose(tile)
             dst[:, 256 * q:256 * q + 128] = turned[0:BLOCK]
             dst[:, 256 * q + 128:256 * q + 256] = turned[BLOCK:]
+
+    order = (1, 6, 0, 7, 2, 5, 3, 4)
+    load.wait()
+    for d in order[:2]:
+        turn_row(dens.at[row_for[d]], stage.at[d])
+    pl.semaphore_wait(barrier, len(greeted))
 
     sends = []
     for d, (dx, dy) in enumerate(DIRS):
@@ -104,9 +112,10 @@
             device_id=at(dx, dy), device_id_type=MESH)
         copy.start()
         sends.append(copy)
-    load.wait()
-    for d, (dx, dy) in enumerate(DIRS):
-        turn_row(dens.at[row_for[d]], stage.at[d])
+    for d in order:
+        dx, dy = DIRS[d]
+        if d not in order[:2]:
+            turn_row(dens.at[row_for[d]], stage.at[d])
         copy = pltpu.make_async_remote_copy(
             src_ref=stage.at[d], dst_ref=mig.at[7 - d], send_sem=mig_send.at[d], recv_sem=mig_recv.at[7 - d],
             device_id=at(dx, dy), device_id_type=MESH)
@@ -120,7 +129,7 @@
     lax.fori_loop(0, ROWS, turn, 0)
 
     flat = jnp.broadcast_to(
-        jnp.concatenate([cols[0, 0, g:g + 1, :] for g in range(ROWS)], axis=1), (8, 128))
+        jnp.concatenate([cols[g:g + 1, :] for g in range(ROWS)], axis=1), (8, 128))
     slot = lax.rem(lax.broadcasted_iota(i32, (8, 128), 1), SLOTS)
     middle = lax.rem(slot, 4)
     place = slot + jnp.where(middle == 1, 1, 0) - jnp.where(middle == 2, 1, 0)
@@ -132,7 +141,7 @@
             found = jnp.where(ids[:, u:u + 1] == flat, PLACE[u], found)
         return found
 
-    tab[0:8, :] = matched(cols[0, 0])
+    tab[0:8, :] = matched(cols[0:ROWS, :])
     for group in range(POOL // 8):
         found = jnp.where(flat == sub + 8 * group, place - SLOTS, 0)
         for width in (1, 2, 4, 8):
@@ -415,16 +424,14 @@
                     chunk = cur[1, g, :, 256 * q + 128 * half:256 * q + 128 * half + 128]
                     tiles.append(2.0 * chunk - chunk_of(pair, odd_row, 2 * q + half))
                 turned = jnp.transpose(jnp.concatenate(tiles, axis=0))
-                dens[g, :, 256 * q:256 * q + 128] = turned[0:BLOCK]
-                dens[g, :, 256 * q + 128:256 * q + 256] = turned[BLOCK:]
+                result[g, :, 256 * q:256 * q + 128] = turned[0:BLOCK]
+                result[g, :, 256 * q + 128:256 * q + 256] = turned[BLOCK:]
         return carry
 
-    lax.fori_loop(0, ROWS // 2, last, 0)
-    write = pltpu.make_async_copy(dens, out_hbm.at[0, 0], out_sem)
-    write.start()
-
+    lax.fori_loop(0, ROWS // 4, last, 0)
     row = exchanged(along_y, sum_y, ny)
     along_x = exchange(row, sum_x, ix, nx, sumx_send, sumx_recv, lambda k: at(k, 0))
+    lax.fori_loop(ROWS // 4, ROWS // 2, last, 0)
     row = exchanged(along_x, sum_x, nx)
     scale = 1.0 / (nx * ny * ROWS * BLOCK)
     for k in range(4):
@@ -434,19 +441,22 @@
         sends[d].wait_send()
     for copy in sends[16:] + along_y + along_x:
         copy.wait_send()
-    write.wait()
 
 
 def shards(nx, ny, density, moves, cols, halo_rows):
+    table = jnp.concatenate([
+        cols.reshape(ROWS, SLOTS),
+        jnp.pad(moves.reshape(1, ROWS), ((0, 0), (0, SLOTS - ROWS))),
+        jnp.pad(halo_rows.reshape(1, HALO), ((0, 0), (0, SLOTS - HALO)))], axis=0)
     dma = pltpu.SemaphoreType.DMA
     vmem = pltpu.VMEM
-    smem_spec = pl.BlockSpec(memory_space=pltpu.SMEM)
-    return pl.pallas_call(
+    result, occupation = pl.pallas_call(
         functools.partial(kernel, nx, ny),
-        out_shape=(jax.ShapeDtypeStruct(density.shape, f32), jax.ShapeDtypeStruct((4,), f32)),
-        in_specs=[smem_spec, smem_spec, pl.BlockSpec(memory_space=vmem), pl.BlockSpec(memory_space=pl.ANY)],
-        out_specs=(pl.BlockSpec(memory_space=pl.ANY), smem_spec),
+        out_shape=(jax.ShapeDtypeStruct((ROWS, BLOCK, STRIP), f32), jax.ShapeDtypeStruct((4,), f32)),
+        in_specs=[pl.BlockSpec(memory_space=vmem), pl.BlockSpec(memory_space=pltpu.HBM)],
+        out_specs=(pl.BlockSpec(memory_space=vmem), pl.BlockSpec(memory_space=pltpu.SMEM)),
         scratch_shapes=[
+            pltpu.SMEM((ROWS + 2, SLOTS), i32),
             vmem((ROWS, BLOCK, STRIP), f32),
             vmem((8, BLOCK, STRIP), f32),
             vmem((8, BLOCK, STRIP), f32),
@@ -470,8 +480,9 @@
             dma((ny,)), dma((ny,)), dma((nx,)), dma((nx,)),
         ],
         compiler_params=pltpu.CompilerParams(
-            collective_id=0, has_side_effects=True, vmem_limit_bytes=60 * 1024 * 1024),
-    )(moves, halo_rows, cols, density)
+            collective_id=0, has_side_effects=True, vmem_limit_bytes=50 * 1024 * 1024),
+    )(table, density)
+    return result.reshape(density.shape), occupation
 
 
 def solution(mesh):

time: 114 us -> 112 us (0.982)
  local copies, waits for them, and re-layouts: 3.68 us -> 1.83 us
    unnamed x4 -> x2, local copies, waits for them, and re-layouts: 3.68 us -> 1.83 us
where the time goes in v4:
time: 112 us
  Pallas kernels  109 us (97%)
  local copies, waits for them, and re-layouts  1.83 us (2%)
    pallas_call x1, Pallas kernels, shards(): pl.pallas_call(functools.partial(kernel, nx, ny), out_shape=(jax.ShapeDty...  109 us

profile of v4, /device:TPU:1, one launch (start us, length us, event | category | flops | bytes accessed | tf_op | source)
XLA Modules:
  0.0 112.2 jit_solution(3911429148054669699)
XLA Ops:
  0.6 0.7 pad_add_fusion.cols
  1.4 109.0 %shard_map.59 = (f32[8,64,1024]{2,1,0:T(8,128)S(1)}, f32[4]{0:T(128)S(1)}) custom-call(s32[10,16]{1,0:T(8,128)S(1)} %pad_add_fusion.cols, f32[1,1,8,64,1024]{4,3,2,1,0:T(8,128)} %dens_hbm.1), custom_call_target="tpu_custom_call" | custom-call | tf_op jit(solution)/shard_map/pallas_call | solution.py:453
  110.4 1.3 %copy.8 = f32[1,1,8,64,1024]{4,3,2,1,0:T(8,128)} copy(f32[1,1,8,64,1024]{4,3,2,1,0:T(8,128)S(1)} %bitcast.4) | data formatting | bytes 4194304
  111.7 0.5 copy.9

commit v5 on v4

--- a/solution.py
+++ b/solution.py
@@ -36,11 +36,17 @@
     ((ZMI, 3), (ZPI, 3), (ZMY, 1), (ZPY, 1)),
     ((ZMY, 2), (ZPY, 2), (ZMY, 3), (ZPY, 3)),
 )
+ARRIVING_LAST = ARRIVING[:5] + (
+    ((ZMI, 2), (ZPI, 2), (ZMY, 1), (ZPY, 1)),
+    ((ZP, 3), (ZPI, 3), (ZMY, 2), (ZMY, 3)),
+    ((ZM, 3), (ZMI, 3), (ZPY, 2), (ZPY, 3)),
+)
+COUNTS = {I: 1, Y: 1, ZM: 0, ZP: 2, ZMI: 0, ZPI: 2, ZMY: 2, ZPY: 0}
 PASS_BEFORE = (0, 2, 4, 5)
 
 
 def kernel(nx, ny, cols, dens_hbm, result, occ_s, cols_s,
-           dens, stage, mig, cur, halo, near, left, prod, acc,
+           dens, stage, mig, cur, halo, near, left, prod, acc, tsum,
            info, infos, tab, tab_s, role_s, parts, sum_y, sum_x,
            local_sem, small_sem, tab_sem, mig_send, mig_recv, info_send, info_recv,
            halo_send, halo_recv, sumy_send, sumy_recv, sumx_send, sumx_recv):
@@ -254,9 +260,20 @@
 
         lax.fori_loop(0, ROWS // 2, one, 0)
 
-    def group(strips, hs, fresh=None):
+    def group(strips, hs, fresh=None, counts=None):
         for k in range(4):
             multiply(strips[k], hs[k], k)
+        if counts is not None:
+            total = tsum[...]
+            for k in range(4):
+                part = None
+                for pair in range(ROWS // 2):
+                    even = prod[k * (SLOTS + 1) + tab_s[hs[k], 2 * SLOTS * pair], pair]
+                    odd = prod[k * (SLOTS + 1) + tab_s[hs[k], 2 * SLOTS * pair + SLOTS], pair]
+                    block = jnp.where(low, even, odd)
+                    part = block if part is None else part + block
+                total = total + counts[k] * part
+            tsum[...] = total
         gather(hs, fresh)
 
     def halo_copy(step, src, role, m, target):
@@ -268,9 +285,11 @@
     def arrival(step, role, m):
         return halo_copy(step, near.at[step, role * HALO + m], role, m, at(0, 1))
 
-    def passed_on(step, m):
+    def passed_on(step, m, roles=(ZM, ZP)):
         out = []
         for role, inside, outside in ((ZM, ZMI, ZMY), (ZP, ZPI, ZPY)):
+            if role not in roles:
+                continue
             src = near.at[step, role * HALO + m]
             if m < HALO - 1:
                 out.append(halo_copy(step, src, outside, m, at(0, cross)))
@@ -281,16 +300,21 @@
         src = near.at[step, Y * HALO + HALO - 1]
         return [halo_copy(step, src, ZPY, HALO - 1, at(-1, 0)), halo_copy(step, src, ZMY, HALO - 1, at(1, 0))]
 
-    def pass_on(step, m):
-        arrival(step, ZM, m).wait_recv()
-        arrival(step, ZP, m).wait_recv()
-        for copy in passed_on(step, m):
+    def pass_on(step, m, roles=(ZM, ZP)):
+        for role in roles:
+            arrival(step, role, m).wait_recv()
+        for copy in passed_on(step, m, roles):
             copy.start()
 
     def pass_on_last(step):
         arrival(step, Y, HALO - 1).wait_recv()
         for copy in passed_on_last(step):
             copy.start()
+        if step == 1:
+            last_along_x(step).start()
+
+    def last_along_x(step):
+        return halo_copy(step, halo.at[step, HALO - 1], ZM, HALO - 1, at(1, 0))
 
     def chunk_of(pair, odd, q):
         first = acc[pair * SLOTS + PLACE[2 * q]]
@@ -321,7 +345,8 @@
                 send(ZP, m, at(-1, 0))
                 send(ZM, m, at(1, 0))
         send(ZP, 3, at(-1, 0))
-        send(ZM, 3, at(1, 0))
+        if step == 0:
+            send(ZM, 3, at(1, 0))
         for m in range(HALO):
             send(I, m, at(0, inner))
 
@@ -340,24 +365,36 @@
             traces.append(before)
 
         def own_group(i, carry):
-            group([cur.at[step, 4 * i + k] for k in range(4)], [4 * i + k for k in range(4)], i == 0)
+            group([cur.at[step, 4 * i + k] for k in range(4)], [4 * i + k for k in range(4)], i == 0,
+                  [1.0] * 4 if step == 1 else None)
             return carry
 
+        if step == 1:
+            tsum[...] = jnp.zeros((BLOCK, 128), f32)
         lax.fori_loop(0, 2, own_group, 0)
 
         def near_strips(q):
             for m in range(HALO):
+                if step == 1 and m == HALO - 1:
+                    for before, role in ((6, ZP), (7, ZM)):
+                        @pl.when(q == before)
+                        def _():
+                            pass_on(step, m, (role,))
+
+                    continue
+
                 @pl.when(q == PASS_BEFORE[m])
                 def _():
                     pass_on(step, m)
                     if m == 0:
                         pass_on_last(step)
 
-            strips, hs = [], []
+            order_of = (ARRIVING, ARRIVING_LAST)[step]
+            strips, hs, counts = [], [], []
             for k in range(4):
-                roles = sum(four[k][0] << (3 * j) for j, four in enumerate(ARRIVING))
-                rows = sum(four[k][1] << (2 * j) for j, four in enumerate(ARRIVING))
-                waits = sum(int(not (four[k][0] in (ZM, ZP) or four[k] == (Y, 3))) << j for j, four in enumerate(ARRIVING))
+                roles = sum(four[k][0] << (3 * j) for j, four in enumerate(order_of))
+                rows = sum(four[k][1] << (2 * j) for j, four in enumerate(order_of))
+                waits = sum(int(not (four[k][0] in (ZM, ZP) or four[k] == (Y, 3))) << j for j, four in enumerate(order_of))
                 role = (jnp.int32(roles) >> (3 * q)) & 7
                 m = (jnp.int32(rows) >> (2 * q)) & 3
 
@@ -367,26 +404,22 @@
 
                 strips.append(near.at[step, role * HALO + m])
                 hs.append(role_s[role] + m)
-            return strips, hs
+                twice = sum(count << (2 * role_) for role_, count in COUNTS.items())
+                counts.append(((jnp.int32(twice) >> (2 * role)) & 3).astype(f32))
+            return strips, hs, None, counts if step == 1 else None
 
         def near_group(q, carry):
             group(*near_strips(q))
             return carry
 
         lax.fori_loop(0, 8 if step == 0 else 7, near_group, 0)
-        if step == 1:
-            strips, hs = near_strips(jnp.int32(7))
-            for k in range(4):
-                multiply(strips[k], hs[k], k)
-            gather(hs, None, range(1))
-
-        total = jnp.zeros((1, 128), f32)
-        for pair in range(ROWS // 2):
-            total = total + trace_of(acc[pair * SLOTS], eye_both)
-        traces.append(total)
+        total = tsum[...] if step == 1 else sum(acc[pair * SLOTS] for pair in range(ROWS // 2))
+        traces.append(trace_of(total, eye_both))
         for m in range(HALO):
             out += passed_on(step, m)
         out += passed_on_last(step)
+        if step == 1:
+            out.append(last_along_x(step))
         sends += out
 
     row = jnp.concatenate([traces[0], traces[1], traces[1], traces[2], jnp.zeros((4, 128), f32)], axis=0)
@@ -413,7 +446,7 @@
 
     along_y = exchange(row, sum_y, iy, ny, sumy_send, sumy_recv, lambda k: at(0, k))
 
-    gather(hs, None, range(1, SLOTS))
+    group(*near_strips(jnp.int32(7))[:2])
 
     def last(pair, carry):
         for odd_row in range(2):
@@ -428,10 +461,9 @@
                 result[g, :, 256 * q + 128:256 * q + 256] = turned[BLOCK:]
         return carry
 
-    lax.fori_loop(0, ROWS // 4, last, 0)
     row = exchanged(along_y, sum_y, ny)
     along_x = exchange(row, sum_x, ix, nx, sumx_send, sumx_recv, lambda k: at(k, 0))
-    lax.fori_loop(ROWS // 4, ROWS // 2, last, 0)
+    lax.fori_loop(0, ROWS // 2, last, 0)
     row = exchanged(along_x, sum_x, nx)
     scale = 1.0 / (nx * ny * ROWS * BLOCK)
     for k in range(4):
@@ -466,6 +498,7 @@
             vmem((ROWS * (SLOTS + 1), 128, 128), bf16),
             vmem((4 * (SLOTS + 1), ROWS // 2, BLOCK, 128), f32),
             vmem((ROWS // 2 * SLOTS, BLOCK, 128), f32),
+            vmem((BLOCK, 128), f32),
             vmem((16, 128), i32),
             vmem((8, 16, 128), i32),
             vmem((2 * POOL + 8, 128), i32),

time: 112 us -> 110 us (0.982)
  Pallas kernels: 109 us -> 106 us
    pallas_call x1, Pallas kernels: 109 us -> 106 us  [shards(): pl.pallas_call(functools.partial(kernel, nx, ny), out_shape=(jax.ShapeDty...]
where the time goes in v5:
time: 110 us; the launch traced here: 109 us
  Pallas kernels  106 us (96%)
  local copies, waits for them, and re-layouts  1.83 us (2%)
    pallas_call x1, Pallas kernels, shards(): pl.pallas_call(functools.partial(kernel, nx, ny), out_shape=(jax.ShapeDty...  106 us

profile of v5, /device:TPU:1, one launch (start us, length us, event | category | flops | bytes accessed | tf_op | source)
XLA Modules:
  0.0 109.5 jit_solution(13280959338405598953)
XLA Ops:
  0.6 0.7 pad_add_fusion.cols
  1.4 106.3 %shard_map.59 = (f32[8,64,1024]{2,1,0:T(8,128)S(1)}, f32[4]{0:T(128)S(1)}) custom-call(s32[10,16]{1,0:T(8,128)S(1)} %pad_add_fusion.cols, f32[1,1,8,64,1024]{4,3,2,1,0:T(8,128)} %dens_hbm.1), custom_call_target="tpu_custom_call" | custom-call | tf_op jit(solution)/shard_map/pallas_call | solution.py:485
  107.6 1.3 %copy.8 = f32[1,1,8,64,1024]{4,3,2,1,0:T(8,128)} copy(f32[1,1,8,64,1024]{4,3,2,1,0:T(8,128)S(1)} %bitcast.4) | data formatting | bytes 4194304
  109.0 0.5 copy.9

commit v6 on v5

--- a/solution.py
+++ b/solution.py
@@ -446,7 +446,12 @@
 
     along_y = exchange(row, sum_y, iy, ny, sumy_send, sumy_recv, lambda k: at(0, k))
 
-    group(*near_strips(jnp.int32(7))[:2])
+    strips, hs = near_strips(jnp.int32(7))[:2]
+    for k in range(4):
+        multiply(strips[k], hs[k], k)
+    row = exchanged(along_y, sum_y, ny)
+    along_x = exchange(row, sum_x, ix, nx, sumx_send, sumx_recv, lambda k: at(k, 0))
+    gather(hs, None)
 
     def last(pair, carry):
         for odd_row in range(2):
@@ -461,8 +466,6 @@
                 result[g, :, 256 * q + 128:256 * q + 256] = turned[BLOCK:]
         return carry
 
-    row = exchanged(along_y, sum_y, ny)
-    along_x = exchange(row, sum_x, ix, nx, sumx_send, sumx_recv, lambda k: at(k, 0))
     lax.fori_loop(0, ROWS // 2, last, 0)
     row = exchanged(along_x, sum_x, nx)
     scale = 1.0 / (nx * ny * ROWS * BLOCK)

time: 110 us -> 110 us (level)
  no operation moved by 1% of the time
where the time goes in v6:
time: 110 us
  Pallas kernels  107 us (97%)
  local copies, waits for them, and re-layouts  1.83 us (2%)
    pallas_call x1, Pallas kernels, shards(): pl.pallas_call(functools.partial(kernel, nx, ny), out_shape=(jax.ShapeDty...  107 us

profile of v6, /device:TPU:1, one launch (start us, length us, event | category | flops | bytes accessed | tf_op | source)
XLA Modules:
  0.0 109.9 jit_solution(5940150100239508814)
XLA Ops:
  0.6 0.7 pad_add_fusion.cols
  1.4 106.7 %shard_map.59 = (f32[8,64,1024]{2,1,0:T(8,128)S(1)}, f32[4]{0:T(128)S(1)}) custom-call(s32[10,16]{1,0:T(8,128)S(1)} %pad_add_fusion.cols, f32[1,1,8,64,1024]{4,3,2,1,0:T(8,128)} %dens_hbm.1), custom_call_target="tpu_custom_call" | custom-call | tf_op jit(solution)/shard_map/pallas_call | solution.py:488
  108.1 1.3 %copy.8 = f32[1,1,8,64,1024]{4,3,2,1,0:T(8,128)} copy(f32[1,1,8,64,1024]{4,3,2,1,0:T(8,128)S(1)} %bitcast.4) | data formatting | bytes 4194304
  109.4 0.5 copy.9
